TPU v7x, 512 devices: a whole 4x4x16 slice. The times are simulated.
512 devices in a mesh: row: 64 (over z, y), col: 8 (over x, core).
Axes of the slice: x: 4, y: 4, z: 16, core: 2. Of those that a mesh axis runs over, the one named last changes fastest.
Arguments:
- acts: bfloat16 [8192, 8192], P('row'), may hold values from -22 to 22
- out_grads: bfloat16 [8192, 4096], P('row', 'col'), may hold values from -0.099436891 to 0.099436891
- weight: float32 [8192, 4096], P('row', 'col'), may hold values from -30 to 30
- row_state: float32 [8192], P('row'), may hold values from 0.002 to 2
- col_state: float32 [4096], P('col'), may hold values from 0.01 to 0.3
Outputs:
- new_weight: float32 [8192, 4096], P('row', 'col')
- update: float32 [8192, 4096], P('row', 'col')
- row_moment: float32 [8192], P('row')
- col_moment: float32 [4096], P('col')
All inputs are finite; a program needn't handle non-finite values.
Results may differ from a plain program's by a relative error of at most 0.0003.
Values may be sent and summed in bfloat16 or wider, within the bound.
A program may use at most 64 MiB of HBM per device.

v0:
```python
import functools

import jax
import jax.numpy as jnp
from jax import lax
from jax.sharding import Mesh
from jax.sharding import PartitionSpec as P

ROW = ("row_0", "row_1")
COL = ("col_0", "col_1")
ROW_COL = ("row_0", "row_1", "col_0", "col_1")


decay_rate = 0.85
floor_eps = 1e-30
relative_rate = 0.05


def copy_for_each(x, axis):
    devices = lax.axis_size(axis)
    return lax.all_to_all(jnp.broadcast_to(x[None], (devices, *x.shape)), axis, 0, 0, tiled=True)


def laid_out(parts, dim):
    dims = list(parts.shape[1:])
    dims[dim] *= parts.shape[0]
    return jnp.moveaxis(parts, 0, dim).reshape(dims)


def gather_directly(x, axis, dim):
    parts = copy_for_each(x, axis)
    return laid_out(parts, dim)


def of_everyone(x, axis):
    return copy_for_each(x, axis).sum(axis=0)


def by_axis(x, axes):
    return functools.reduce(lax.psum, axes, x)


def per_device(acts, out_grads, weight, row_state, col_state):
    n_row = lax.axis_size(ROW)
    n_col = lax.axis_size(COL)
    tok_dev = acts.shape[0]
    width = acts.shape[1]
    rows_here = width // n_row
    cols_here = out_grads.shape[1]
    cols_all = cols_here * n_col
    share_rows = tok_dev // n_col
    own_rows = lax.dynamic_slice_in_dim(acts, lax.axis_index(COL) * share_rows, share_rows, 0)
    arrived = lax.all_to_all(own_rows, ROW, split_axis=1, concat_axis=0, tiled=True)
    arrived = arrived.reshape(n_row, share_rows, rows_here)
    columns = gather_directly(arrived, COL, 1).reshape(n_row * tok_dev, rows_here)
    gradient = lax.dot_general(
        columns,
        lax.all_gather(out_grads, ROW, axis=0, tiled=True),
        (((0,), (0,)), ((), ())),
        preferred_element_type=jnp.float32,
    )
    squares = gradient * gradient + floor_eps
    row_squares = jnp.sum(squares, axis=1)
    col_squares = jnp.sum(squares, axis=0)
    weight_part = jnp.sum(weight * weight)
    row_total = lax.psum(row_squares, COL)
    col_total = of_everyone(col_squares, ROW)
    weight_total = by_axis(weight_part, ROW_COL)
    row_moment = decay_rate * row_state + (1.0 - decay_rate) * (row_total / cols_all)
    col_moment = decay_rate * col_state + (1.0 - decay_rate) * (col_total / width)
    unclipped = gradient * lax.rsqrt(row_moment[:, None] * col_moment[None, :])
    update_total = by_axis(jnp.sum(unclipped * unclipped), ROW_COL)
    count_all = width * cols_all
    clip_factor = jnp.maximum(1.0, jnp.sqrt(update_total / count_all))
    update = unclipped / clip_factor
    step_size = relative_rate * jnp.sqrt(weight_total / count_all + 1e-06)
    new_weight = weight - step_size * update
    return (new_weight, update, row_moment, col_moment)


def solution(mesh):
    finer = Mesh(mesh.devices.reshape(16, 4, 4, 2), ("row_0", "row_1", "col_0", "col_1"))
    placed = (P(ROW, None), P(ROW, COL), P(ROW, COL), P(ROW), P(COL))
    return jax.shard_map(
        per_device,
        mesh=finer,
        in_specs=placed,
        out_specs=(P(ROW, COL), P(ROW, COL), P(ROW), P(COL)),
        check_vma=False,
    )
```

profile of v0, /device:TPU:1, one launch (start us, length us, event | category | flops | bytes accessed | tf_op | source)
XLA Modules:
  0.0 268.2 jit_solution(16159256373061868356)
XLA Ops:
  7.2 0.0 copy-start
  7.2 0.0 all-gather.2.cloned.1.call-start
  7.2 0.7 all-gather.2.cloned.1.call-update
  7.9 0.8 copy-done
  8.8 39.6 %all_to_all.27 = bf16[16,64,128]{2,0,1:T(8,128)(2,1)S(1)} all-to-all(bf16[16,64,128]{2,0,1:T(8,128)(2,1)S(1)} %copy_bitcast_fusion), channel_id=1, replica_groups=mesh['row_0'=16,'row_1'=4,'col_0'=4,'col_1'=2] {'row_0','row_1'}, dimensions={1} | all-to-all | bytes 524288 | tf_op jit(solution)/shard_map/all_to_all | solution.py:53
  48.4 0.3 broadcast_in_dim.4
  48.7 34.3 %all_to_all.28 = bf16[8,64,16,128]{3,2,1,0:T(8,128)(2,1)S(1)} all-to-all(bf16[8,64,16,128]{3,2,1,0:T(8,128)(2,1)S(1)} %broadcast_in_dim.4), channel_id=1, replica_groups=mesh['row_0'=16,'row_1'=4,'col_0'=4,'col_1'=2] {'col_0','col_1'}, dimensions={0} | all-to-all | bytes 4194304 | tf_op jit(solution)/shard_map/all_to_all | solution.py:21
  83.0 2.0 copy.15
  85.0 81.7 %all-gather.2.cloned.1.call-done = bf16[8192,512]{1,0:T(8,128)(2,1)} async-done(((bf16[128,512]{1,0:T(8,128)(2,1)}), bf16[8192,512]{1,0:T(8,128)(2,1)}) %all-gather.2.cloned.1.call-update) | async-done | bytes 8388624 | tf_op jit(solution)/shard_map/all_gather | solution.py:58
  166.8 0.0 copy-start.1
  166.8 0.0 copy-start.5
  166.8 0.0 copy-start.4
  166.8 5.4 %fusion.1 = (f32[128]{0:T(128)S(1)}, f32[512]{0:T(512)S(1)}, f32[128,512]{1,0:T(8,128)S(1)}) fusion(bf16[8192,128]{1,0:T(8,128)(2,1)} %bitcast.11, bf16[8192,512]{1,0:T(8,128)(2,1)} %all-gather.2.cloned.1.call-done), kind=kOutput, calls=%fused_computation.8 | convolution fusion | flops 1074003328 | bytes 10750464 | tf_op jit(solution)/shard_map/dot_general | solution.py:56
  172.2 0.7 broadcast_in_dim.5
  172.9 8.7 %all-to-all-start.2 = ((f32[64,1,512]{2,1,0:T(1,128)}), f32[64,1,512]{2,1,0:T(1,128)S(1)}, u32[]{:S(2)}, u32[]{:S(2)}) async-start(f32[64,1,512]{2,1,0:T(1,128)} %broadcast_in_dim.5), calls=%async_computation.2 | async-start | bytes 262144 | tf_op jit(solution)/shard_map/all_to_all | solution.py:21
  181.6 0.0 copy-done.1
  181.6 0.7 multiply_reduce_fusion.1
  182.3 20.9 %psum.67 = f32[128]{0:T(128)S(1)} all-reduce(f32[128]{0:T(128)S(1)} %get-tuple-element.4), channel_id=1, replica_groups=mesh['row_0'=16,'row_1'=4,'col_0'=4,'col_1'=2] {'col_0','col_1'}, use_global_device_ids=true, to_apply=%region_6.0 | all-reduce | flops 128 | bytes 1024 | tf_op jit(solution)/shard_map/psum | solution.py:66
  203.2 0.0 copy-done.5
  203.2 0.0 copy-start.3
  203.2 0.0 all-to-all-done.2
  203.2 0.1 reduce_sum.48
  203.3 0.0 copy-done.4
  203.4 0.0 copy-start.2
  203.4 0.8 multiply_reduce_fusion
  204.1 24.2 %all-reduce = (f32[]{:T(128)}, f32[]{:T(128)}) all-reduce(f32[]{:T(128)} %multiply_reduce_fusion, f32[]{:T(128)} %multiply_reduce_fusion.1), channel_id=1, replica_groups=mesh['row_0'=16,'row_1'=4,'col_0'=4,'col_1'=2] {'row_0'}, use_global_device_ids=true, to_apply=%region_10.0 | all-reduce | flops 2 | bytes 16 | tf_op jit(solution)/shard_map/psum | solution.py:40
  228.4 8.8 %all-reduce.2 = (f32[]{:T(128)}, f32[]{:T(128)}) all-reduce(f32[]{:T(128)} %get-tuple-element.6, f32[]{:T(128)} %get-tuple-element.7), channel_id=1, replica_groups=mesh['row_0'=16,'row_1'=4,'col_0'=4,'col_1'=2] {'row_1'}, use_global_device_ids=true, to_apply=%region_11.0 | all-reduce | flops 2 | bytes 16 | tf_op jit(solution)/shard_map/psum | solution.py:40
  237.1 6.9 %all-reduce.1 = (f32[]{:T(128)}, f32[]{:T(128)}) all-reduce(f32[]{:T(128)} %get-tuple-element.10, f32[]{:T(128)} %get-tuple-element.11), channel_id=1, replica_groups=mesh['row_0'=16,'row_1'=4,'col_0'=4,'col_1'=2] {'col_0'}, use_global_device_ids=true, to_apply=%region_12.0 | all-reduce | flops 2 | bytes 16 | tf_op jit(solution)/shard_map/psum | solution.py:40
  244.0 15.0 %all-reduce.3 = (f32[]{:T(128)}, f32[]{:T(128)}) all-reduce(f32[]{:T(128)} %get-tuple-element.8, f32[]{:T(128)} %get-tuple-element.9), channel_id=1, replica_groups=mesh['row_0'=16,'row_1'=4,'col_0'=4,'col_1'=2] {'col_1'}, use_global_device_ids=true, to_apply=%region_13.0 | all-reduce | flops 2 | bytes 16 | tf_op jit(solution)/shard_map/psum | solution.py:40
  260.4 0.9 multiply_subtract_fusion
  261.3 0.0 copy-done.3
  261.3 0.0 copy-done.2
  (3 shorter events, 0.1 us)
Async XLA Ops:
  7.2 1.6 copy-start
  7.2 159.6 %all-gather.2.cloned.1.call-start = ((), (), s32[]{:S(2)}) async-start(), calls=%async_computation.3 | async-start | bytes 8519680 | tf_op jit(solution)/shard_map/all_gather | solution.py:58
  166.8 14.9 %copy-start.1 = (f32[128,512]{1,0:T(8,128)S(1)}, f32[128,512]{1,0:T(8,128)}, u32[]{:S(2)}) copy-start(f32[128,512]{1,0:T(8,128)} %param.7) | copy-start | bytes 786436
  166.8 36.4 %copy-start.5 = (f32[128]{0:T(128)S(1)}, f32[128]{0:T(128)}, u32[]{:S(2)}) copy-start(f32[128]{0:T(128)} %param.8) | copy-start | bytes 1540
  166.8 36.6 %copy-start.4 = (f32[512]{0:T(512)S(1)}, f32[512]{0:T(512)}, u32[]{:S(2)}) copy-start(f32[512]{0:T(512)} %param.9) | copy-start | bytes 6148
  172.9 30.3 %all-to-all-start.2 = ((f32[64,1,512]{2,1,0:T(1,128)}), f32[64,1,512]{2,1,0:T(1,128)S(1)}, u32[]{:S(2)}, u32[]{:S(2)}) async-start(f32[64,1,512]{2,1,0:T(1,128)} %broadcast_in_dim.5), calls=%async_computation.2 | async-start | bytes 262144 | tf_op jit(solution)/shard_map/all_to_all | solution.py:21
  203.2 58.1 %copy-start.3 = (f32[128]{0:T(128)}, f32[128]{0:T(128)S(1)}, u32[]{:S(2)}) copy-start(f32[128]{0:T(128)S(1)} %multiply_add_fusion.2) | copy-start | bytes 1540
  203.4 58.0 %copy-start.2 = (f32[512]{0:T(512)}, f32[512]{0:T(512)S(1)}, u32[]{:S(2)}) copy-start(f32[512]{0:T(512)S(1)} %multiply_add_fusion.1) | copy-start | bytes 6148
Sparse Core Ops, SparseCore 0:
  11.0 155.7 all-gather.1
where the time goes:
time: 269 us; the launch traced here: 268 us
  blocking collectives  150 us (56%)
  waiting for transfers between devices  82.4 us (31%)
  between operations  15.5 us (6%)
  starting transfers between devices  8.72 us (3%)
  matrix products  5.43 us (2%)
  local copies, waits for them, and re-layouts  3.92 us (1%)
    all_gather x1, waiting for transfers between devices, per_device(): lax.all_gather(out_grads, ROW, axis=0, tiled=True)  81.7 us
    psum x4, blocking collectives, by_axis(): return functools.reduce(lax.psum, axes, x)  54.9 us
    all_to_all x1, blocking collectives, per_device(): lax.all_to_all(own_rows, ROW, split_axis=1, concat_axis=0, tiled=True)  39.6 us
    all_to_all x1, blocking collectives, copy_for_each(): lax.all_to_all(jnp.broadcast_to(x[None], (devices, *x.shape)), axis, 0, 0...  34.3 us
    psum x1, blocking collectives, per_device(): row_total = lax.psum(row_squares, COL)  20.9 us
    all_to_all x1, starting transfers between devices, copy_for_each(): lax.all_to_all(jnp.broadcast_to(x[None], (devices, *x.shape)), axis, 0, 0...  8.68 us
    dot_general x1, matrix products, per_device(): lax.dot_general(columns, lax.all_gather(out_grads, ROW, axis=0, tiled=Tru...  5.43 us
  transfers between devices with their start and end apart: 2, of which 1 were waited for; matrix products, arithmetic and copies ran while one was open for 1% of the time, Pallas kernels for 0%

commit v1 on v0

v1 whole, which is shorter than its diff:
```python
import jax
import jax.numpy as jnp
from jax import lax
from jax.sharding import Mesh
from jax.sharding import PartitionSpec as P

Z, Y = "row_0", "row_1"
ROW = (Z, Y)
COL = ("col_0", "col_1")

decay_rate = 0.85
floor_eps = 1e-30
relative_rate = 0.05


def per_device(acts, out_grads, weight, row_state, col_state):
    n_row = lax.axis_size(ROW)
    n_z = lax.axis_size(Z)
    n_y = lax.axis_size(Y)
    n_col = lax.axis_size(COL)
    tok_dev = acts.shape[0]
    width = acts.shape[1]
    cols_here = out_grads.shape[1]
    cols_all = cols_here * n_col
    share_rows = tok_dev // n_col
    own_rows = lax.dynamic_slice_in_dim(acts, lax.axis_index(COL) * share_rows, share_rows, 0)
    arrived = lax.all_to_all(own_rows, Z, split_axis=1, concat_axis=0, tiled=True)
    columns = lax.all_gather(arrived.reshape(n_z, share_rows, width // n_z), COL, axis=1, tiled=True)
    columns = columns.reshape(n_z * tok_dev, width // n_z)
    gathered = lax.all_gather(out_grads, Z, axis=0, tiled=True)
    partial = lax.dot_general(
        columns, gathered, (((0,), (0,)), ((), ())), preferred_element_type=jnp.float32
    )
    gradient = lax.psum_scatter(partial, Y, scatter_dimension=0, tiled=True)
    squares = gradient * gradient + floor_eps
    row_squares = jnp.sum(squares, axis=1)
    col_squares = jnp.sum(squares, axis=0)
    weight_part = jnp.sum(weight * weight)
    row_total = lax.psum(row_squares, COL)
    row_moment = decay_rate * row_state + (1.0 - decay_rate) * (row_total / cols_all)
    scaled = gradient * lax.rsqrt(row_moment)[:, None]
    stacked = jnp.concatenate([col_squares, jnp.sum(scaled * scaled, axis=0)])
    stacked = lax.psum(stacked, ROW)
    col_total, scaled_total = stacked[:cols_here], stacked[cols_here:]
    col_moment = decay_rate * col_state + (1.0 - decay_rate) * (col_total / width)
    unclipped = gradient * lax.rsqrt(row_moment[:, None] * col_moment[None, :])
    update_total = lax.psum(jnp.sum(scaled_total / col_moment), COL)
    weight_total = lax.psum(weight_part, ROW + COL)
    count_all = width * cols_all
    clip_factor = jnp.maximum(1.0, jnp.sqrt(update_total / count_all))
    update = unclipped / clip_factor
    step_size = relative_rate * jnp.sqrt(weight_total / count_all + 1e-06)
    new_weight = weight - step_size * update
    return (new_weight, update, row_moment, col_moment)


def solution(mesh):
    finer = Mesh(mesh.devices.reshape(16, 4, 4, 2), (Z, Y) + COL)
    placed = (P(ROW, None), P(ROW, COL), P(ROW, COL), P(ROW), P(COL))
    return jax.shard_map(
        per_device,
        mesh=finer,
        in_specs=placed,
        out_specs=(P(ROW, COL), P(ROW, COL), P(ROW), P(COL)),
        check_vma=False,
    )
```

time: 269 us -> 433 us (1.61)
  blocking collectives: 150 us -> 305 us
  waiting for transfers between devices: 82.4 us -> 96 us
  starting transfers between devices: 8.72 us -> 0.12 us
    psum x4 -> x3, blocking collectives: 54.9 us -> 264 us  [the longest x1 112 us: per_device(): stacked = lax.psum(stacked, ROW)]
    all_to_all x2 -> x1, blocking collectives: 73.9 us -> 28.7 us  [per_device(): lax.all_to_all(own_rows, Z, split_axis=1, concat_axis=0, tiled=True)]
    all_gather x1 -> x2, waiting for transfers between devices: 81.7 us -> 95.2 us  [the longest x1 62.1 us: per_device(): gathered = lax.all_gather(out_grads, Z, axis=0, tiled=True)]
    all_to_all x1 -> x0, starting transfers between devices: 8.68 us -> none  [copy_for_each(): lax.all_to_all(jnp.broadcast_to(x[None], (devices, *x.shape)), axis, 0, 0...]
    psum x1, blocking collectives: 20.9 us -> 12.4 us  [per_device(): row_total = lax.psum(row_squares, COL)]
  transfers between devices with their start and end apart: 2 -> 3, of which waited for: 1 -> 2; matrix products, arithmetic and copies ran while one was open for 1% -> 1% of each run, Pallas kernels for 0% -> 0%
where the time goes in v1:
time: 433 us; the launch traced here: 432 us
  blocking collectives  305 us (70%)
  waiting for transfers between devices  96 us (22%)
  between operations  15.2 us (4%)
  local copies, waits for them, and re-layouts  6.49 us (1%)
  other arithmetic  5.28 us (1%)
  matrix products  4.51 us (1%)
    psum x1, blocking collectives, per_device(): stacked = lax.psum(stacked, ROW)  112 us
    psum x1, blocking collectives, per_device(): weight_total = lax.psum(weight_part, ROW + COL)  111 us
    all_gather x1, waiting for transfers between devices, per_device(): gathered = lax.all_gather(out_grads, Z, axis=0, tiled=True)  62.1 us
    psum x1, blocking collectives, per_device(): update_total = lax.psum(jnp.sum(scaled_total / col_moment), COL)  40.8 us
    all_gather x1, waiting for transfers between devices, per_device(): lax.all_gather(arrived.reshape(n_z, share_rows, width // n_z), COL, axis=...  33.2 us
    all_to_all x1, blocking collectives, per_device(): lax.all_to_all(own_rows, Z, split_axis=1, concat_axis=0, tiled=True)  28.7 us
    psum x1, blocking collectives, per_device(): row_total = lax.psum(row_squares, COL)  12.4 us
  transfers between devices with their start and end apart: 3, of which 2 were waited for; matrix products, arithmetic and copies ran while one was open for 1% of the time, Pallas kernels for 0%

profile of v1, /device:TPU:1, one launch (start us, length us, event | category | flops | bytes accessed | tf_op | source)
XLA Modules:
  0.0 432.5 jit_solution(11988476071683671557)
XLA Ops:
  7.2 0.0 copy-start
  7.2 0.0 all-gather.3.cloned.1.call-start
  7.2 1.5 copy-done
  8.8 28.7 %all_to_all.16 = bf16[16,16,512]{2,0,1:T(8,128)(2,1)S(1)} all-to-all(bf16[16,16,512]{2,0,1:T(8,128)(2,1)S(1)} %bitcast.10), channel_id=1, replica_groups=mesh['row_0'=16,'row_1'=4,'col_0'=4,'col_1'=2] {'row_0'}, dimensions={1} | all-to-all | bytes 524288 | tf_op jit(solution)/shard_map/all_to_all | solution.py:27
  37.5 0.9 copy.11
  38.3 0.0 all-gather.3.cloned.1.call-update
  38.4 0.0 all-gather.5.cloned.1.call-start
  38.4 0.7 all-gather.5.cloned.1.call-update
  39.1 0.0 reduce-scatter.2.cloned.1.call-start
  39.2 33.2 %all-gather.3.cloned.1.call-done = bf16[16,128,512]{2,0,1:T(8,128)(2,1)} async-done(((bf16[16,16,512]{2,0,1:T(8,128)(2,1)}), bf16[16,128,512]{2,0,1:T(8,128)(2,1)}) %all-gather.3.cloned.1.call-update) | async-done | bytes 2097168 | tf_op jit(solution)/shard_map/all_gather | solution.py:28
  72.3 4.0 copy.12
  76.4 62.1 %all-gather.5.cloned.1.call-done = bf16[2048,512]{1,0:T(8,128)(2,1)} async-done(((bf16[128,512]{1,0:T(8,128)(2,1)}), bf16[2048,512]{1,0:T(8,128)(2,1)}) %all-gather.5.cloned.1.call-update) | async-done | bytes 2097168 | tf_op jit(solution)/shard_map/all_gather | solution.py:30
  138.5 0.0 copy-start.1
  138.5 0.0 copy-start.5
  138.5 0.0 copy-start.4
  138.5 4.5 %fusion.4 = f32[512,512]{1,0:T(8,128)} fusion(bf16[2048,512]{1,0:T(8,128)(2,1)} %bitcast.8, bf16[2048,512]{1,0:T(8,128)(2,1)} %all-gather.5.cloned.1.call-done), kind=kOutput, calls=%fused_computation.15 | convolution fusion | flops 1073741824 | bytes 5242880 | tf_op jit(solution)/shard_map/dot_general | solution.py:31
  143.0 0.0 reduce-scatter.2.cloned.1.call-update
  143.0 0.0 copy-done.1
  143.0 0.7 multiply_reduce_fusion.1
  143.7 110.9 %psum.28 = f32[]{:T(128)} all-reduce(f32[]{:T(128)} %multiply_reduce_fusion.1), channel_id=1, replica_groups=mesh['row_0'=16,'row_1'=4,'col_0'=4,'col_1'=2] {'row_0','row_1','col_0',..., use_global_device_ids=true, to_apply=%region_1.0 | all-reduce | flops 1 | bytes 8 | tf_op jit(solution)/shard_map/psum | solution.py:48
  255.2 0.0 reduce-scatter.2.cloned.1.call-done
  255.3 1.1 fusion.1
  256.3 12.4 %psum.29 = f32[128]{0:T(128)S(1)} all-reduce(f32[128]{0:T(128)S(1)} %fusion.1), channel_id=1, replica_groups=mesh['row_0'=16,'row_1'=4,'col_0'=4,'col_1'=2] {'col_0','col_1'}, use_global_device_ids=true, to_apply=%region_4.0 | all-reduce | flops 128 | bytes 1024 | tf_op jit(solution)/shard_map/psum | solution.py:39
  268.8 0.0 copy-done.5
  268.8 0.0 copy-start.3
  268.8 1.1 fusion
  269.9 112.1 %psum.30 = f32[1024]{0:T(1024)S(1)} all-reduce(f32[1024]{0:T(1024)S(1)} %pad_maximum_fusion), channel_id=1, replica_groups=mesh['row_0'=16,'row_1'=4,'col_0'=4,'col_1'=2] {'row_0','row_1'}, use_global_device_ids=true, to_apply=%region_7.0 | all-reduce | flops 1024 | bytes 8192 | tf_op jit(solution)/shard_map/psum | solution.py:43
  382.0 0.0 copy-done.4
  382.0 0.6 fusion.2
  382.6 0.0 copy-start.2
  382.6 40.8 %psum.31 = f32[]{:T(128)} all-reduce(f32[]{:T(128)} %get-tuple-element.8), channel_id=1, replica_groups=mesh['row_0'=16,'row_1'=4,'col_0'=4,'col_1'=2] {'col_0','col_1'}, use_global_device_ids=true, to_apply=%region_9.0 | all-reduce | flops 1 | bytes 8 | tf_op jit(solution)/shard_map/psum | solution.py:47
  424.1 1.9 multiply_subtract_fusion
  425.9 0.0 copy-done.3
  426.0 0.0 copy-done.2
  (4 shorter events, 0.1 us)
Async XLA Ops:
  7.2 1.6 copy-start
  7.2 65.1 %all-gather.3.cloned.1.call-start = ((), (), s32[]{:S(2)}) async-start(), calls=%async_computation.2 | async-start | bytes 2359296 | tf_op jit(solution)/shard_map/all_gather | solution.py:28
  38.4 100.1 %all-gather.5.cloned.1.call-start = ((), (), s32[]{:S(2)}) async-start(), calls=%async_computation.3 | async-start | bytes 2228224 | tf_op jit(solution)/shard_map/all_gather | solution.py:30
  39.1 216.1 %reduce-scatter.2.cloned.1.call-start = ((), (), s32[]{:S(2)}) async-start(), calls=%async_computation.4 | async-start | bytes 1310720 | tf_op jit(solution)/shard_map/reduce_scatter | solution.py:34
  138.5 4.5 %copy-start.1 = (f32[128,512]{1,0:T(8,128)S(1)}, f32[128,512]{1,0:T(8,128)}, u32[]{:S(2)}) copy-start(f32[128,512]{1,0:T(8,128)} %param.7) | copy-start | bytes 786436
  138.5 130.3 %copy-start.5 = (f32[128]{0:T(128)S(1)}, f32[128]{0:T(128)}, u32[]{:S(2)}) copy-start(f32[128]{0:T(128)} %param.8) | copy-start | bytes 1540
  138.5 243.5 %copy-start.4 = (f32[512]{0:T(512)S(1)}, f32[512]{0:T(512)}, u32[]{:S(2)}) copy-start(f32[512]{0:T(512)} %param.9) | copy-start | bytes 6148
  268.8 157.2 %copy-start.3 = (f32[128]{0:T(128)}, f32[128]{0:T(128)S(1)}, u32[]{:S(2)}) copy-start(f32[128]{0:T(128)S(1)} %get-tuple-element.11) | copy-start | bytes 1540
  382.6 43.4 %copy-start.2 = (f32[512]{0:T(512)}, f32[512]{0:T(512)S(1)}, u32[]{:S(2)}) copy-start(f32[512]{0:T(512)S(1)} %get-tuple-element.9) | copy-start | bytes 6148
Sparse Core Ops, SparseCore 0:
  38.5 33.7 all-gather.2
  74.4 64.0 all-gather.4
  143.1 36.4 reduce-scatter.1

commit v2 on v1

v2 whole, which is shorter than its diff:
```python
import functools

import jax
import jax.numpy as jnp
from jax import lax
from jax.experimental import pallas as pl
from jax.experimental.pallas import tpu as pltpu
from jax.sharding import Mesh
from jax.sharding import PartitionSpec as P

Z, Y, X, C = "z", "y", "x", "c"
ROW = (Z, Y)
COL = (X, C)
LANE = 128

decay_rate = 0.85
floor_eps = 1e-30
relative_rate = 0.05


def kernel(
    sizes,
    acts, og, weight, row_state, col_state,
    grad_out, row_out, col_out, scal_out,
    A, G, part, R, wv, rs_v, cs_v, st1, st2, st3, st4,
    local_sem, a2a_send, a2a_recv, x_send, x_recv, d_send, d_recv,
    ring_send, ring_recv, y_send, y_recv, st_send, st_recv,
):
    nz, ny, nx, nc, tok, cols, width = sizes
    half = nz // 2
    groups = cols // LANE
    rows_z = ny * LANE
    share = tok // (nx * nc)
    core_rows = share * nx
    cols_all = cols * nx * nc
    z, y, x, c = (lax.axis_index(a) for a in (Z, Y, X, C))
    xc = x * nc + c
    own = c * core_rows + x * share

    def to_z(d):
        return lax.rem(z + d, nz)

    def remote(src, dst, send, recv, where):
        return pltpu.make_async_remote_copy(
            src_ref=src, dst_ref=dst, send_sem=send, recv_sem=recv,
            device_id=where, device_id_type=pl.DeviceIdType.MESH,
        )

    def wait_bytes(ref, sem):
        pltpu.make_async_copy(ref, ref, sem).wait()

    def col_peer(k):
        i = lax.rem(xc + k, nx * nc)
        return {X: i // nc, C: lax.rem(i, nc)}

    barrier = pltpu.get_barrier_semaphore()
    for d in range(1, nz):
        pl.semaphore_signal(barrier, inc=1, device_id={Z: to_z(d)}, device_id_type=pl.DeviceIdType.MESH)
    for d in range(1, ny):
        pl.semaphore_signal(barrier, inc=1, device_id={Y: lax.rem(y + d, ny)}, device_id_type=pl.DeviceIdType.MESH)
    for k in range(1, nx * nc):
        pl.semaphore_signal(barrier, inc=1, device_id=col_peer(k), device_id_type=pl.DeviceIdType.MESH)

    own_cols = pl.ds(pl.multiple_of(z * rows_z, LANE), rows_z)
    local = [
        pltpu.make_async_copy(acts.at[:, own_cols], A.at[0, 0], local_sem.at[0]),
        pltpu.make_async_copy(og, G.at[0, 0], local_sem.at[1]),
        pltpu.make_async_copy(weight, wv, local_sem.at[2]),
        pltpu.make_async_copy(row_state, rs_v, local_sem.at[3]),
        pltpu.make_async_copy(col_state, cs_v, local_sem.at[4]),
    ]
    for copy in local:
        copy.start()
    part[...] = jnp.zeros_like(part)
    pl.semaphore_wait(barrier, nz - 1 + ny - 1 + nx * nc - 1)

    own_rows = pl.ds(pl.multiple_of(own, share), share)

    def send_acts(target, p, q, send, recv):
        there = pl.ds(pl.multiple_of(target * rows_z, LANE), rows_z)
        remote(acts.at[own_rows, there], A.at[p, q, own_rows, :], send, recv, {Z: target}).start()

    def send_pair(h, carry):
        send_acts(to_z(h), h, 0, a2a_send.at[0], a2a_recv.at[h])
        send_acts(to_z(nz - h), h, 1, a2a_send.at[0], a2a_recv.at[h])
        return carry

    lax.fori_loop(1, half, send_pair, 0)
    send_acts(to_z(half), 0, 1, a2a_send.at[1], a2a_recv.at[0])

    for copy in local:
        copy.wait()

    def last_hop(way, g):
        return half if (g < groups // 2) == (way == 0) else half - 1

    def ring_sem(way, g):
        return ring_send.at[way, 0 if last_hop(way, g) == half else 1]

    def lanes(g):
        return pl.ds(g * LANE, LANE)

    def ring_copy(way, g, h):
        src = G.at[h, way, :, lanes(g)] if not isinstance(h, int) else G.at[0, 0, :, lanes(g)]
        nxt = h + 1
        q = nxt // half if way == 0 else 1
        return remote(
            src, G.at[lax.rem(nxt, half), q, :, lanes(g)], ring_sem(way, g), ring_recv.at[way, g, h],
            {Z: to_z(1 if way == 0 else nz - 1)},
        )

    def x_pair(p):
        for d in range(1, nx):
            there = {X: lax.rem(x + d, nx)}
            mine = A.at[p, :, own_rows, :]
            remote(mine, mine, x_send.at[0], x_recv.at[p], there).start()

    def x_last():
        for d in range(1, nx):
            there = {X: lax.rem(x + d, nx)}
            mine = A.at[0, 1, own_rows, :]
            remote(mine, mine, x_send.at[1], x_recv.at[0], there).start()

    core_part = pl.ds(pl.multiple_of(c * core_rows, core_rows), core_rows)
    sibling = {C: nc - 1 - c}

    def step(s, carry):
        for g in range(groups):
            @pl.when(s == g + 1)
            def _():
                for way in range(2):
                    ring_copy(way, g, 0).start()

        r = s - 2
        for g in range(groups):
            h = r - g
            for way in range(2):
                last = last_hop(way, g)

                @pl.when(jnp.logical_and(h >= 1, h <= last))
                def _():
                    wait_bytes(G.at[0, 0, :, lanes(g)], ring_recv.at[way, g, h - 1])

                @pl.when(jnp.logical_and(h >= 1, h < last))
                def _():
                    ring_copy(way, g, h).start()

        @pl.when(s < half)
        def _():
            wait_bytes(A.at[0, :, pl.ds(0, share), :], a2a_recv.at[s])
            x_pair(s)

        @pl.when(s == half)
        def _():
            wait_bytes(A.at[0, 0, pl.ds(0, share), :], a2a_recv.at[0])
            x_last()

        @pl.when(jnp.logical_and(s >= 2, s <= half))
        def _():
            wait_bytes(A.at[0, :, pl.ds(0, share * (nx - 1)), :], x_recv.at[s - 1])
            mine = A.at[s - 1, :, core_part, :]
            remote(mine, mine, d_send.at[0], d_recv.at[s - 1], sibling).start()

        @pl.when(s == half + 1)
        def _():
            wait_bytes(A.at[0, 0, pl.ds(0, share * (nx - 1)), :], x_recv.at[0])
            mine = A.at[0, 1, core_part, :]
            remote(mine, mine, d_send.at[1], d_recv.at[0], sibling).start()

        @pl.when(jnp.logical_and(s >= 3, s <= half + 1))
        def _():
            wait_bytes(A.at[0, :, pl.ds(0, core_rows), :], d_recv.at[s - 2])

        @pl.when(s == half + 2)
        def _():
            wait_bytes(A.at[0, 0, pl.ds(0, core_rows), :], d_recv.at[0])

        for g in range(groups):
            h = r - g

            @pl.when(jnp.logical_and(h >= 1, h <= half))
            def _():
                p = lax.rem(h, half)
                grads = G[p, :, :, g * LANE:(g + 1) * LANE].reshape(2 * tok, LANE)
                block = A[p].reshape(2 * tok, rows_z)
                product = lax.dot_general(
                    grads, block, (((0,), (0,)), ((), ())), preferred_element_type=jnp.float32
                )
                for yy in range(ny):
                    part[g, yy] += product[:, yy * LANE:(yy + 1) * LANE]

            @pl.when(h == half)
            def _():
                for d in range(1, ny):
                    there = lax.rem(y + d, ny)
                    remote(part.at[g, there], R.at[g, d - 1], y_send.at[0], y_recv.at[g], {Y: there}).start()

        return carry

    lax.fori_loop(1, half + groups + 2, step, 0)

    weight_sq = jnp.sum(wv[...] * wv[...], axis=0, keepdims=True)
    weight_sq = sum(weight_sq[:, g * LANE:(g + 1) * LANE] for g in range(groups))

    row_sq = jnp.zeros((1, LANE), jnp.float32)
    for g in range(groups):
        wait_bytes(R.at[0], y_recv.at[g])
        total = part[g, y]
        for d in range(ny - 1):
            total += R[g, d]
        row_sq += jnp.sum(total * total + floor_eps, axis=0, keepdims=True)
        grad_out[:, g * LANE:(g + 1) * LANE] = total.T

    st1[xc] = jnp.broadcast_to(row_sq, (8, LANE))
    for k in range(1, nx * nc):
        remote(st1.at[xc], st1.at[xc], st_send.at[0], st_recv.at[0], col_peer(k)).start()
    for g in range(groups):
        grads = grad_out[:, g * LANE:(g + 1) * LANE]
        st2[y, g:g + 1, :] = jnp.sum(grads * grads + floor_eps, axis=0, keepdims=True)
    st2[y, 8:16, :] = jnp.broadcast_to(weight_sq, (8, LANE))
    wait_bytes(A.at[pl.ds(0, half - 1), :, pl.ds(0, share), :], a2a_send.at[0])
    wait_bytes(A.at[0, 0, pl.ds(0, share), :], a2a_send.at[1])
    wait_bytes(A.at[pl.ds(0, half - 1), :, pl.ds(0, share * (nx - 1)), :], x_send.at[0])
    wait_bytes(A.at[0, 0, pl.ds(0, share * (nx - 1)), :], x_send.at[1])
    wait_bytes(A.at[pl.ds(0, half - 1), :, pl.ds(0, core_rows), :], d_send.at[0])
    wait_bytes(A.at[0, 0, pl.ds(0, core_rows), :], d_send.at[1])
    for way in range(2):
        wait_bytes(G.at[:, 0, :, pl.ds(0, cols // 2)], ring_send.at[way, 0])
        wait_bytes(G.at[pl.ds(0, half - 1), 0, :, pl.ds(0, cols // 2)], ring_send.at[way, 1])
    wait_bytes(part.at[:, pl.ds(0, ny - 1)], y_send.at[0])

    wait_bytes(st1.at[pl.ds(0, nx * nc - 1)], st_recv.at[0])
    row_total = st1[0, 0:1, :]
    for k in range(1, nx * nc):
        row_total += st1[k, 0:1, :]
    row_moment = decay_rate * rs_v[...] + (1.0 - decay_rate) * (row_total / cols_all)
    row_out[...] = row_moment
    inverse = jnp.broadcast_to(1.0 / row_moment, (LANE, LANE)).T
    for g in range(groups):
        grads = grad_out[:, g * LANE:(g + 1) * LANE]
        st2[y, 4 + g:5 + g, :] = jnp.sum(grads * grads * inverse, axis=0, keepdims=True)

    for d in range(1, ny):
        remote(st2.at[y], st2.at[y], st_send.at[1], st_recv.at[1], {Y: lax.rem(y + d, ny)}).start()
    wait_bytes(st1.at[pl.ds(0, nx * nc - 1)], st_send.at[0])
    wait_bytes(st2.at[pl.ds(0, ny - 1)], st_recv.at[1])
    over_y = st2[0]
    for d in range(1, ny):
        over_y += st2[d]
    st3[z] = over_y
    for d in range(1, nz):
        remote(st3.at[z], st3.at[z], st_send.at[2], st_recv.at[2], {Z: to_z(d)}).start()
    wait_bytes(st2.at[pl.ds(0, ny - 1)], st_send.at[1])
    wait_bytes(st3.at[pl.ds(0, nz - 1)], st_recv.at[2])
    over_z = st3[0]
    for d in range(1, nz):
        over_z += st3[d]
    col_moment = decay_rate * cs_v[...] + (1.0 - decay_rate) * (over_z[0:groups] / width)
    col_out[...] = col_moment
    st4[xc, 0:4, :] = over_z[4:4 + groups] / col_moment
    st4[xc, 4:8, :] = over_z[8:12]

    for k in range(1, nx * nc):
        remote(st4.at[xc], st4.at[xc], st_send.at[3], st_recv.at[3], col_peer(k)).start()
    wait_bytes(st3.at[pl.ds(0, nz - 1)], st_send.at[2])
    wait_bytes(st4.at[pl.ds(0, nx * nc - 1)], st_recv.at[3])
    over_x = st4[0]
    for k in range(1, nx * nc):
        over_x += st4[k]
    scal_out[0:1, :] = jnp.broadcast_to(jnp.sum(over_x[0:4], keepdims=True), (1, LANE))
    scal_out[1:2, :] = jnp.broadcast_to(jnp.sum(over_x[4:5], keepdims=True), (1, LANE))
    wait_bytes(st4.at[pl.ds(0, nx * nc - 1)], st_send.at[3])


def per_device(acts, out_grads, weight, row_state, col_state):
    nz, ny, nx, nc = (lax.axis_size(a) for a in (Z, Y, X, C))
    tok, width = acts.shape
    cols = out_grads.shape[1]
    groups = cols // LANE
    half = nz // 2
    rows_z = ny * LANE
    anywhere = pl.BlockSpec(memory_space=pl.ANY)
    vmem = pl.BlockSpec(memory_space=pltpu.VMEM)
    f32 = jnp.float32
    gradient, row_moment, col_moment, scalars = pl.pallas_call(
        functools.partial(kernel, (nz, ny, nx, nc, tok, cols, width)),
        out_shape=(
            jax.ShapeDtypeStruct((LANE, cols), f32),
            jax.ShapeDtypeStruct((1, LANE), f32),
            jax.ShapeDtypeStruct((groups, LANE), f32),
            jax.ShapeDtypeStruct((8, LANE), f32),
        ),
        in_specs=[anywhere] * 5,
        out_specs=[vmem] * 4,
        scratch_shapes=[
            pltpu.VMEM((half, 2, tok, rows_z), jnp.bfloat16),
            pltpu.VMEM((half, 2, tok, cols), jnp.bfloat16),
            pltpu.VMEM((groups, ny, LANE, LANE), f32),
            pltpu.VMEM((groups, ny - 1, LANE, LANE), f32),
            pltpu.VMEM((LANE, cols), f32),
            pltpu.VMEM((1, LANE), f32),
            pltpu.VMEM((groups, LANE), f32),
            pltpu.VMEM((nx * nc, 8, LANE), f32),
            pltpu.VMEM((ny, 16, LANE), f32),
            pltpu.VMEM((nz, 16, LANE), f32),
            pltpu.VMEM((nx * nc, 8, LANE), f32),
            pltpu.SemaphoreType.DMA((5,)),
            pltpu.SemaphoreType.DMA((2,)),
            pltpu.SemaphoreType.DMA((half,)),
            pltpu.SemaphoreType.DMA((2,)),
            pltpu.SemaphoreType.DMA((half,)),
            pltpu.SemaphoreType.DMA((2,)),
            pltpu.SemaphoreType.DMA((half,)),
            pltpu.SemaphoreType.DMA((2, 2)),
            pltpu.SemaphoreType.DMA((2, groups, half)),
            pltpu.SemaphoreType.DMA((1,)),
            pltpu.SemaphoreType.DMA((groups,)),
            pltpu.SemaphoreType.DMA((4,)),
            pltpu.SemaphoreType.DMA((4,)),
        ],
        compiler_params=pltpu.CompilerParams(
            collective_id=0, has_side_effects=True, vmem_limit_bytes=32 * 1024 * 1024
        ),
    )(acts, out_grads, weight, row_state.reshape(1, LANE), col_state.reshape(groups, LANE))
    count_all = width * cols * nx * nc
    row_moment = row_moment.reshape(-1)
    col_moment = col_moment.reshape(-1)
    clip_factor = jnp.maximum(1.0, jnp.sqrt(scalars[0, 0] / count_all))
    step_size = relative_rate * jnp.sqrt(scalars[1, 0] / count_all + 1e-06)
    unclipped = gradient * lax.rsqrt(row_moment[:, None] * col_moment[None, :])
    update = unclipped / clip_factor
    new_weight = weight - step_size * update
    return (new_weight, update, row_moment, col_moment)


def solution(mesh):
    finer = Mesh(mesh.devices.reshape(16, 4, 4, 2), (Z, Y, X, C))
    return jax.shard_map(
        per_device,
        mesh=finer,
        in_specs=(P(ROW, None), P(ROW, COL), P(ROW, COL), P(ROW), P(COL)),
        out_specs=(P(ROW, COL), P(ROW, COL), P(ROW), P(COL)),
        check_vma=False,
    )
```

time: 433 us -> 102 us (0.24)
  blocking collectives: 305 us -> 0 us
  waiting for transfers between devices: 96 us -> 0 us
  Pallas kernels: 0 us -> 92.3 us
  between operations: 15.2 us -> 2.04 us
  matrix products: 4.51 us -> 0 us
  other arithmetic: 5.28 us -> 0.92 us
    psum x4 -> x0, blocking collectives: 276 us -> none  [the longest x1 112 us: per_device(): stacked = lax.psum(stacked, ROW)]
    all_gather x2 -> x0, waiting for transfers between devices: 95.2 us -> none  [the longest x1 62.1 us: per_device(): gathered = lax.all_gather(out_grads, Z, axis=0, tiled=True)]
    pallas_call x0 -> x1, Pallas kernels: none -> 92.3 us  [per_device(): pl.pallas_call(functools.partial(kernel, (nz, ny, nx, nc, tok, cols, widt...]
    all_to_all x1 -> x0, blocking collectives: 28.7 us -> none  [per_device(): lax.all_to_all(own_rows, Z, split_axis=1, concat_axis=0, tiled=True)]
    dot_general x1 -> x0, matrix products: 4.51 us -> none  [per_device(): lax.dot_general(columns, gathered, (((0,), (0,)), ((), ())), preferred_el...]
  transfers between devices with their start and end apart: 3 -> 0, of which waited for: 2 -> 0; matrix products, arithmetic and copies ran while one was open for 1% -> 0% of each run, Pallas kernels for 0% -> 0%
where the time goes in v2:
time: 102 us
  Pallas kernels  92.3 us (90%)
  local copies, waits for them, and re-layouts  6.38 us (6%)
  between operations  2.04 us (2%)
    pallas_call x1, Pallas kernels, per_device(): pl.pallas_call(functools.partial(kernel, (nz, ny, nx, nc, tok, cols, widt...  92.3 us
    unnamed x12, local copies, waits for them, and re-layouts  5.86 us

profile of v2, /device:TPU:1, one launch (start us, length us, event | category | flops | bytes accessed | tf_op | source)
XLA Modules:
  0.0 101.6 jit_solution(9879388343427118249)
XLA Ops:
  0.6 0.0 copy-start
  0.6 1.6 %copy-done = bf16[128,8192]{1,0:T(8,128)(2,1)S(1)} copy-done((bf16[128,8192]{1,0:T(8,128)(2,1)S(1)}, bf16[128,8192]{1,0:T(8,128)(2,1)}, u32[]{:S(2)}) %copy-start) | copy-done | bytes 2097176
  2.2 0.0 copy-start.1
  2.2 0.9 copy-done.1
  3.2 0.0 copy-start.2
  3.2 0.9 copy-done.2
  4.1 0.0 copy-start.3
  4.1 0.7 copy-done.3
  4.8 0.0 copy-start.4
  4.8 0.7 copy-done.4
  5.4 92.3 %shard_map.84 = (f32[128,512]{1,0:T(8,128)S(1)}, f32[1,128]{1,0:T(1,128)S(1)}, f32[4,128]{1,0:T(4,128)S(1)}, f32[8,128]{1,0:T(8,128)S(1)}) custom-call(bf16[128,8192]{1,0:T(8,128)(2,1)S(1)} %copy-done, bf16[128,512]{1,0:T(8,128)(2,1)S(1)} %copy-done.2, f32[128,512]{1,0:T(8,128)S(1)} %copy-done.1, f32[1,128]{1,0:T(1,128)S(1)} %bitcast.9, f32[4,128]{1,0:T(4,128)S(1)} %bitcast.8), custom_call_target="tpu_custom_call" | custom-call | tf_op jit(solution)/shard_map/pallas_call | solution.py:285
  97.7 0.5 fusion
  99.6 0.9 multiply_subtract_fusion
  100.5 0.5 copy.11
  101.0 0.6 copy.12
Async XLA Ops:
  0.6 1.6 %copy-start = (bf16[128,8192]{1,0:T(8,128)(2,1)S(1)}, bf16[128,8192]{1,0:T(8,128)(2,1)}, u32[]{:S(2)}) copy-start(bf16[128,8192]{1,0:T(8,128)(2,1)} %acts.1) | copy-start | bytes 6291460
  2.2 0.9 copy-start.1
  3.2 0.9 copy-start.2
  4.1 0.7 copy-start.3
  4.8 0.7 copy-start.4

commit v3 on v2

v3 whole, which is shorter than its diff:
```python
import functools

import jax
import jax.numpy as jnp
from jax import lax
from jax.experimental import pallas as pl
from jax.experimental.pallas import tpu as pltpu
from jax.sharding import Mesh
from jax.sharding import PartitionSpec as P

Z, Y, X, C = "z", "y", "x", "c"
ROW = (Z, Y)
COL = (X, C)
LANE = 128
LAG = (0, 0, 1, 1)
BATCHES = (([0, 1], 2), ([2, 3], 3), ([4, 5], 4), ([6], 5), ([7], 5))

decay_rate = 0.85
floor_eps = 1e-30
relative_rate = 0.05


def plan(half, groups, lag, batches):
    steps = [("first", g) for g in range(groups) if lag[g] == 0]
    steps.append(("acts",))
    steps += [("first", g) for g in range(groups) if lag[g] == 1]
    ready, done = [], {g: [] for g in range(groups)}
    arrived = {g: [] for g in range(groups)}
    for r in range(1, half + max(lag) + 1):
        for g in range(groups):
            if lag[g] == r and r > 1:
                steps.append(("first", g))
            h = r - lag[g]
            if 1 <= h <= half:
                steps.append(("hop", g, h))
                arrived[g].append(h - 1)
        for stage in (1, 2, 3):
            for pairs, at in batches:
                if at + stage - 1 == r:
                    steps.append(("pairs", stage, pairs))
                    if stage == 3:
                        ready += pairs
        for g in range(groups):
            todo = [i for i in arrived[g] if i in ready and i not in done[g]]
            done[g] += todo
            if todo:
                steps.append(("dot", g, todo))
            if r - lag[g] == half:
                assert len(done[g]) == half
                steps.append(("scatter", g))
    return steps


def kernel(
    sizes,
    acts, og, weight, row_state, col_state,
    unclipped_out, row_out, col_out, clip_out, step_out,
    A, G, part, R, grad, wv, rs_v, cs_v, st1, st2, st3, st4,
    local_sem, a2a_send, a2a_recv, x_send, x_recv, d_send, d_recv,
    ring_send, ring_recv, y_send, y_recv, st_send, st_recv,
):
    nz, ny, nx, nc, tok, cols, width = sizes
    half = nz // 2
    groups = cols // LANE
    rows_z = ny * LANE
    share = tok // (nx * nc)
    core_rows = share * nx
    cols_all = cols * nx * nc
    count_all = width * cols_all
    z, y, x, c = (lax.axis_index(a) for a in (Z, Y, X, C))
    xc = x * nc + c
    own = c * core_rows + x * share
    far = half - 1

    def to_z(d):
        return lax.rem(z + d, nz)

    def remote(src, dst, send, recv, where):
        return pltpu.make_async_remote_copy(
            src_ref=src, dst_ref=dst, send_sem=send, recv_sem=recv,
            device_id=where, device_id_type=pl.DeviceIdType.MESH,
        )

    def wait_bytes(ref, sem):
        pltpu.make_async_copy(ref, ref, sem).wait()

    def col_peer(k):
        i = lax.rem(xc + k, nx * nc)
        return {X: i // nc, C: lax.rem(i, nc)}

    own_cols = pl.ds(pl.multiple_of(z * rows_z, LANE), rows_z)
    local = [
        pltpu.make_async_copy(og.at[:, pl.ds(g * LANE, LANE)], G.at[g, far, 0], local_sem.at[g])
        for g in range(groups)
    ] + [
        pltpu.make_async_copy(acts.at[:, own_cols], A.at[far, 0], local_sem.at[groups]),
        pltpu.make_async_copy(weight, wv, local_sem.at[groups + 1]),
        pltpu.make_async_copy(row_state, rs_v, local_sem.at[groups + 2]),
        pltpu.make_async_copy(col_state, cs_v, local_sem.at[groups + 3]),
    ]

    barrier = pltpu.get_barrier_semaphore()
    for d in sorted(range(1, nz), key=lambda d: -min(d, nz - d)):
        pl.semaphore_signal(barrier, inc=1, device_id={Z: to_z(d)}, device_id_type=pl.DeviceIdType.MESH)
    for d in range(1, ny):
        pl.semaphore_signal(barrier, inc=1, device_id={Y: lax.rem(y + d, ny)}, device_id_type=pl.DeviceIdType.MESH)
    for k in range(1, nx * nc):
        pl.semaphore_signal(barrier, inc=1, device_id=col_peer(k), device_id_type=pl.DeviceIdType.MESH)
    for copy in local:
        copy.start()
    for copy in local:
        copy.wait()
    weight_sq = jnp.sum(wv[...] * wv[...], axis=0, keepdims=True)
    weight_sq = sum(weight_sq[:, g * LANE:(g + 1) * LANE] for g in range(groups))
    st2[y, 8:16, :] = jnp.broadcast_to(weight_sq, (8, LANE))
    pl.semaphore_wait(barrier, nz - 1 + ny - 1 + nx * nc - 1)

    own_rows = pl.ds(pl.multiple_of(own, share), share)
    core_part = pl.ds(pl.multiple_of(c * core_rows, core_rows), core_rows)
    sibling = {C: nc - 1 - c}

    def send_acts(target, i, q, send, recv):
        there = pl.ds(pl.multiple_of(target * rows_z, LANE), rows_z)
        remote(acts.at[own_rows, there], A.at[i, q, own_rows, :], send, recv, {Z: target}).start()

    def last_hop(way, g):
        return half if (g % 2 == 0) == (way == 0) else half - 1

    def ring_copy(way, g, h):
        src = G.at[g, h - 1, way] if h else G.at[g, far, 0]
        q = 1 if h + 1 == half else way
        return remote(
            src, G.at[g, h, q], ring_send.at[way, 0 if last_hop(way, g) == half else 1],
            ring_recv.at[way, g, h], {Z: to_z(1 if way == 0 else nz - 1)},
        )

    def pairs_stage(stage, pairs):
        i, n = pairs[0], len(pairs)
        if pairs == [far]:
            block, kind = (lambda rows: A.at[far, 1, rows, :]), 1
        else:
            block, kind = (lambda rows: A.at[pl.ds(i, n), :, rows, :]), 0
        if stage == 1:
            for j in pairs:
                wait_bytes(A.at[far, 1, pl.ds(0, share), :] if kind else A.at[0, :, pl.ds(0, share), :], a2a_recv.at[j])
            for d in range(1, nx):
                remote(block(own_rows), block(own_rows), x_send.at[kind], x_recv.at[i], {X: lax.rem(x + d, nx)}).start()
        elif stage == 2:
            wait_bytes(block(pl.ds(0, share * (nx - 1))), x_recv.at[i])
            remote(block(core_part), block(core_part), d_send.at[kind], d_recv.at[i], sibling).start()
        else:
            wait_bytes(block(pl.ds(0, core_rows)), d_recv.at[i])

    started = set()
    for what, *of in plan(half, groups, LAG, BATCHES):
        if what == "first":
            for way in range(2):
                ring_copy(way, of[0], 0).start()
        elif what == "acts":
            for h in range(1, half):
                send_acts(to_z(h), h - 1, 0, a2a_send.at[0], a2a_recv.at[h - 1])
                send_acts(to_z(nz - h), h - 1, 1, a2a_send.at[0], a2a_recv.at[h - 1])
            send_acts(to_z(half), far, 1, a2a_send.at[1], a2a_recv.at[far])
        elif what == "hop":
            g, h = of
            for way in range(2):
                if h <= last_hop(way, g):
                    wait_bytes(G.at[g, 0, 0], ring_recv.at[way, g, h - 1])
                if h < last_hop(way, g):
                    ring_copy(way, g, h).start()
        elif what == "pairs":
            pairs_stage(*of)
        elif what == "dot":
            g, todo = of
            for i in todo:
                product = lax.dot_general(
                    G[g, i].reshape(2 * tok, LANE), A[i].reshape(2 * tok, rows_z),
                    (((0,), (0,)), ((), ())), preferred_element_type=jnp.float32,
                )
                for yy in range(ny):
                    block = product[:, yy * LANE:(yy + 1) * LANE]
                    part[g, yy] = part[g, yy] + block if g in started else block
                started.add(g)
        elif what == "scatter":
            g = of[0]
            for d in range(1, ny):
                there = lax.rem(y + d, ny)
                remote(part.at[g, there], R.at[g, d - 1], y_send.at[0], y_recv.at[g], {Y: there}).start()

    row_sq = jnp.zeros((1, LANE), jnp.float32)
    for g in range(groups):
        wait_bytes(R.at[0], y_recv.at[g])
        total = part[g, y]
        for d in range(ny - 1):
            total += R[g, d]
        row_sq += jnp.sum(total * total + floor_eps, axis=0, keepdims=True)
        grad[:, g * LANE:(g + 1) * LANE] = total.T

    st1[xc] = jnp.broadcast_to(row_sq, (8, LANE))
    for k in range(1, nx * nc):
        remote(st1.at[xc], st1.at[xc], st_send.at[0], st_recv.at[0], col_peer(k)).start()
    for g in range(groups):
        grads = grad[:, g * LANE:(g + 1) * LANE]
        st2[y, g:g + 1, :] = jnp.sum(grads * grads + floor_eps, axis=0, keepdims=True)
    wait_bytes(A.at[pl.ds(0, half - 1), :, pl.ds(0, share), :], a2a_send.at[0])
    wait_bytes(A.at[0, 0, pl.ds(0, share), :], a2a_send.at[1])
    wait_bytes(A.at[pl.ds(0, half - 1), :, pl.ds(0, share * (nx - 1)), :], x_send.at[0])
    wait_bytes(A.at[0, 0, pl.ds(0, share * (nx - 1)), :], x_send.at[1])
    wait_bytes(A.at[pl.ds(0, half - 1), :, pl.ds(0, core_rows), :], d_send.at[0])
    wait_bytes(A.at[0, 0, pl.ds(0, core_rows), :], d_send.at[1])
    for way in range(2):
        wait_bytes(G.at[0], ring_send.at[way, 0])
        wait_bytes(G.at[0, pl.ds(0, half - 1)], ring_send.at[way, 1])
    wait_bytes(part.at[:, pl.ds(0, ny - 1)], y_send.at[0])

    wait_bytes(st1.at[pl.ds(0, nx * nc - 1)], st_recv.at[0])
    row_total = st1[0, 0:1, :]
    for k in range(1, nx * nc):
        row_total += st1[k, 0:1, :]
    row_moment = decay_rate * rs_v[...] + (1.0 - decay_rate) * (row_total / cols_all)
    row_out[...] = row_moment
    rows_down = jnp.broadcast_to(row_moment, (LANE, LANE)).T
    inverse = 1.0 / rows_down
    for g in range(groups):
        grads = grad[:, g * LANE:(g + 1) * LANE]
        st2[y, 4 + g:5 + g, :] = jnp.sum(grads * grads * inverse, axis=0, keepdims=True)

    for d in range(1, ny):
        remote(st2.at[y], st2.at[y], st_send.at[1], st_recv.at[1], {Y: lax.rem(y + d, ny)}).start()
    wait_bytes(st1.at[pl.ds(0, nx * nc - 1)], st_send.at[0])
    wait_bytes(st2.at[pl.ds(0, ny - 1)], st_recv.at[1])
    over_y = st2[0]
    for d in range(1, ny):
        over_y += st2[d]
    st3[z] = over_y
    for d in sorted(range(1, nz), key=lambda d: -min(d, nz - d)):
        remote(st3.at[z], st3.at[z], st_send.at[2], st_recv.at[2], {Z: to_z(d)}).start()
    wait_bytes(st2.at[pl.ds(0, ny - 1)], st_send.at[1])
    wait_bytes(st3.at[pl.ds(0, nz - 1)], st_recv.at[2])
    over_z = st3[0]
    for d in range(1, nz):
        over_z += st3[d]
    col_moment = decay_rate * cs_v[...] + (1.0 - decay_rate) * (over_z[0:groups] / width)
    st4[xc, 0:4, :] = over_z[4:4 + groups] / col_moment
    st4[xc, 4:8, :] = over_z[8:12]

    for k in range(1, nx * nc):
        remote(st4.at[xc], st4.at[xc], st_send.at[3], st_recv.at[3], col_peer(k)).start()
    col_out[...] = col_moment
    for g in range(groups):
        lanes = slice(g * LANE, (g + 1) * LANE)
        unclipped_out[:, lanes] = grad[:, lanes] * lax.rsqrt(rows_down * col_moment[g:g + 1, :])
    wait_bytes(st3.at[pl.ds(0, nz - 1)], st_send.at[2])
    wait_bytes(st4.at[pl.ds(0, nx * nc - 1)], st_recv.at[3])
    over_x = st4[0]
    for k in range(1, nx * nc):
        over_x += st4[k]
    update_total = jnp.sum(over_x[0:4], keepdims=True)
    weight_total = jnp.sum(over_x[4:5], keepdims=True)
    clip_out[...] = jnp.broadcast_to(jnp.maximum(1.0, jnp.sqrt(update_total / count_all)), clip_out.shape)
    step_out[...] = jnp.broadcast_to(relative_rate * jnp.sqrt(weight_total / count_all + 1e-06), step_out.shape)
    wait_bytes(st4.at[pl.ds(0, nx * nc - 1)], st_send.at[3])


def per_device(acts, out_grads, weight, row_state, col_state):
    nz, ny, nx, nc = (lax.axis_size(a) for a in (Z, Y, X, C))
    tok, width = acts.shape
    cols = out_grads.shape[1]
    groups = cols // LANE
    half = nz // 2
    rows_z = ny * LANE
    anywhere = pl.BlockSpec(memory_space=pl.ANY)
    vmem = pl.BlockSpec(memory_space=pltpu.VMEM)
    f32 = jnp.float32
    unclipped, row_moment, col_moment, clip_factor, step_size = pl.pallas_call(
        functools.partial(kernel, (nz, ny, nx, nc, tok, cols, width)),
        out_shape=(
            jax.ShapeDtypeStruct((LANE, cols), f32),
            jax.ShapeDtypeStruct((1, LANE), f32),
            jax.ShapeDtypeStruct((groups, LANE), f32),
            jax.ShapeDtypeStruct((groups, LANE), f32),
            jax.ShapeDtypeStruct((groups, LANE), f32),
        ),
        in_specs=[anywhere] * 5,
        out_specs=[vmem] * 5,
        scratch_shapes=[
            pltpu.VMEM((half, 2, tok, rows_z), jnp.bfloat16),
            pltpu.VMEM((groups, half, 2, tok, LANE), jnp.bfloat16),
            pltpu.VMEM((groups, ny, LANE, LANE), f32),
            pltpu.VMEM((groups, ny - 1, LANE, LANE), f32),
            pltpu.VMEM((LANE, cols), f32),
            pltpu.VMEM((LANE, cols), f32),
            pltpu.VMEM((1, LANE), f32),
            pltpu.VMEM((groups, LANE), f32),
            pltpu.VMEM((nx * nc, 8, LANE), f32),
            pltpu.VMEM((ny, 16, LANE), f32),
            pltpu.VMEM((nz, 16, LANE), f32),
            pltpu.VMEM((nx * nc, 8, LANE), f32),
            pltpu.SemaphoreType.DMA((groups + 4,)),
            pltpu.SemaphoreType.DMA((2,)),
            pltpu.SemaphoreType.DMA((half,)),
            pltpu.SemaphoreType.DMA((2,)),
            pltpu.SemaphoreType.DMA((half,)),
            pltpu.SemaphoreType.DMA((2,)),
            pltpu.SemaphoreType.DMA((half,)),
            pltpu.SemaphoreType.DMA((2, 2)),
            pltpu.SemaphoreType.DMA((2, groups, half)),
            pltpu.SemaphoreType.DMA((1,)),
            pltpu.SemaphoreType.DMA((groups,)),
            pltpu.SemaphoreType.DMA((4,)),
            pltpu.SemaphoreType.DMA((4,)),
        ],
        compiler_params=pltpu.CompilerParams(
            collective_id=0, has_side_effects=True, vmem_limit_bytes=60 * 1024 * 1024
        ),
    )(acts, out_grads, weight, row_state.reshape(1, LANE), col_state.reshape(groups, LANE))
    update = unclipped / clip_factor.reshape(1, -1)
    new_weight = weight - step_size.reshape(1, -1) * update
    return (new_weight, update, row_moment.reshape(-1), col_moment.reshape(-1))


def solution(mesh):
    finer = Mesh(mesh.devices.reshape(16, 4, 4, 2), (Z, Y, X, C))
    return jax.shard_map(
        per_device,
        mesh=finer,
        in_specs=(P(ROW, None), P(ROW, COL), P(ROW, COL), P(ROW), P(COL)),
        out_specs=(P(ROW, COL), P(ROW, COL), P(ROW), P(COL)),
        check_vma=False,
    )
```

time: 102 us -> 94.4 us (0.925)
  local copies, waits for them, and re-layouts: 6.38 us -> 2.38 us
  Pallas kernels: 92.3 us -> 89.4 us
  between operations: 2.04 us -> 0.66 us
    unnamed x12 -> x4, local copies, waits for them, and re-layouts: 5.86 us -> 2.38 us
    pallas_call x1, Pallas kernels: 92.3 us -> 89.4 us  [per_device(): pl.pallas_call(functools.partial(kernel, (nz, ny, nx, nc, tok, cols, widt...]
where the time goes in v3:
time: 94.4 us; the launch traced here: 94.3 us
  Pallas kernels  89.4 us (95%)
  local copies, waits for them, and re-layouts  2.38 us (3%)
  other arithmetic  1.82 us (2%)
    pallas_call x1, Pallas kernels, per_device(): pl.pallas_call(functools.partial(kernel, (nz, ny, nx, nc, tok, cols, widt...  89.4 us
    unnamed x4, local copies, waits for them, and re-layouts  2.38 us

profile of v3, /device:TPU:1, one launch (start us, length us, event | category | flops | bytes accessed | tf_op | source)
XLA Modules:
  0.0 94.3 jit_solution(4192031928992303859)
XLA Ops:
  0.6 0.0 copy-start
  0.6 89.4 %shard_map.84 = (f32[128,512]{1,0:T(8,128)}, f32[1,128]{1,0:T(1,128)}, f32[4,128]{1,0:T(4,128)}, f32[4,128]{1,0:T(4,128)}, f32[4,128]{1,0:T(4,128)}) custom-call(bf16[128,8192]{1,0:T(8,128)(2,1)} %acts.1, bf16[128,512]{1,0:T(8,128)(2,1)} %og.1, f32[128,512]{1,0:T(8,128)} %weight.1, f32[1,128]{1,0:T(1,128)} %bitcast.10, f32[4,128]{1,0:T(4,128)} %bitcast.6), custom_call_target="tpu_custom_call" | custom-call | tf_op jit(solution)/shard_map/pallas_call | solution.py:275
  90.1 0.0 copy-done
  90.1 1.8 %multiply_subtract_fusion = (f32[128,512]{1,0:T(8,128)}, f32[128,512]{1,0:T(8,128)}) fusion(f32[128,512]{1,0:T(8,128)S(1)} %copy-done, f32[512]{0:T(512)} %bitcast.8, f32[128,512]{1,0:T(8,128)} %get-tuple-element.10, f32[512]{0:T(512)} %bitcast.7), kind=kLoop, calls=%fused_computation | loop fusion | flops 196608 | bytes 1052672 | tf_op jit(solution)/shard_map/sub | solution.py:318
  91.9 1.1 %copy.11 = f32[128]{0:T(128)} copy(f32[128]{0:T(128)} %bitcast.11) | data formatting | bytes 1024
  93.0 1.3 %copy.12 = f32[512]{0:T(512)} copy(f32[512]{0:T(512)} %bitcast.9) | data formatting | bytes 4096
Async XLA Ops:
  0.6 89.4 %copy-start = (f32[128,512]{1,0:T(8,128)S(1)}, f32[128,512]{1,0:T(8,128)}, u32[]{:S(2)}) copy-start(f32[128,512]{1,0:T(8,128)} %weight.1) | copy-start | bytes 786436

commit v4 on v3

--- a/solution.py
+++ b/solution.py
@@ -13,16 +13,18 @@
 COL = (X, C)
 LANE = 128
 LAG = (0, 0, 1, 1)
-BATCHES = (([0, 1], 2), ([2, 3], 3), ([4, 5], 4), ([6], 5), ([7], 5))
+SENDS = (([7], 0), ([6, 5], 0), ([4, 3], 1), ([2, 1, 0], 2))
+BATCHES = (([7], 2), ([5, 6], 2), ([3, 4], 3), ([0, 1, 2], 4))
 
 decay_rate = 0.85
 floor_eps = 1e-30
 relative_rate = 0.05
 
 
-def plan(half, groups, lag, batches):
+def plan(half, groups, lag, sends, batches):
     steps = [("first", g) for g in range(groups) if lag[g] == 0]
-    steps.append(("acts",))
+    steps += [("acts", pairs) for pairs, at in sends if at == 0]
+    steps.append(("weights",))
     steps += [("first", g) for g in range(groups) if lag[g] == 1]
     ready, done = [], {g: [] for g in range(groups)}
     arrived = {g: [] for g in range(groups)}
@@ -34,6 +36,7 @@
             if 1 <= h <= half:
                 steps.append(("hop", g, h))
                 arrived[g].append(h - 1)
+        steps += [("acts", pairs) for pairs, at in sends if at == r]
         for stage in (1, 2, 3):
             for pairs, at in batches:
                 if at + stage - 1 == r:
@@ -55,7 +58,7 @@
     sizes,
     acts, og, weight, row_state, col_state,
     unclipped_out, row_out, col_out, clip_out, step_out,
-    A, G, part, R, grad, wv, rs_v, cs_v, st1, st2, st3, st4,
+    A, G, part, R, grad, wv, rs_v, cs_v, st1, st2, st3, st4, wy, wz,
     local_sem, a2a_send, a2a_recv, x_send, x_recv, d_send, d_recv,
     ring_send, ring_recv, y_send, y_recv, st_send, st_recv,
 ):
@@ -84,9 +87,14 @@
     def wait_bytes(ref, sem):
         pltpu.make_async_copy(ref, ref, sem).wait()
 
+    ys = sorted(range(1, ny), key=lambda d: -min(d, ny - d))
+    xs = sorted(range(1, nx), key=lambda d: -min(d, nx - d))
+    zs = sorted(range(1, nz), key=lambda d: -min(d, nz - d))
+    peers = [(d, e) for d in xs for e in range(nc)] + [(0, e) for e in range(1, nc)]
+
     def col_peer(k):
-        i = lax.rem(xc + k, nx * nc)
-        return {X: i // nc, C: lax.rem(i, nc)}
+        d, e = k
+        return {X: lax.rem(x + d, nx), C: lax.rem(c + e, nc)}
 
     own_cols = pl.ds(pl.multiple_of(z * rows_z, LANE), rows_z)
     local = [
@@ -100,11 +108,11 @@
     ]
 
     barrier = pltpu.get_barrier_semaphore()
-    for d in sorted(range(1, nz), key=lambda d: -min(d, nz - d)):
+    for d in zs:
         pl.semaphore_signal(barrier, inc=1, device_id={Z: to_z(d)}, device_id_type=pl.DeviceIdType.MESH)
     for d in range(1, ny):
         pl.semaphore_signal(barrier, inc=1, device_id={Y: lax.rem(y + d, ny)}, device_id_type=pl.DeviceIdType.MESH)
-    for k in range(1, nx * nc):
+    for k in peers:
         pl.semaphore_signal(barrier, inc=1, device_id=col_peer(k), device_id_type=pl.DeviceIdType.MESH)
     for copy in local:
         copy.start()
@@ -112,7 +120,7 @@
         copy.wait()
     weight_sq = jnp.sum(wv[...] * wv[...], axis=0, keepdims=True)
     weight_sq = sum(weight_sq[:, g * LANE:(g + 1) * LANE] for g in range(groups))
-    st2[y, 8:16, :] = jnp.broadcast_to(weight_sq, (8, LANE))
+    wy[y] = weight_sq
     pl.semaphore_wait(barrier, nz - 1 + ny - 1 + nx * nc - 1)
 
     own_rows = pl.ds(pl.multiple_of(own, share), share)
@@ -143,7 +151,7 @@
         if stage == 1:
             for j in pairs:
                 wait_bytes(A.at[far, 1, pl.ds(0, share), :] if kind else A.at[0, :, pl.ds(0, share), :], a2a_recv.at[j])
-            for d in range(1, nx):
+            for d in xs:
                 remote(block(own_rows), block(own_rows), x_send.at[kind], x_recv.at[i], {X: lax.rem(x + d, nx)}).start()
         elif stage == 2:
             wait_bytes(block(pl.ds(0, share * (nx - 1))), x_recv.at[i])
@@ -151,18 +159,37 @@
         else:
             wait_bytes(block(pl.ds(0, core_rows)), d_recv.at[i])
 
+    def weights_over_y():
+        for d in range(1, ny):
+            remote(wy.at[y], wy.at[y], st_send.at[4], st_recv.at[4], {Y: lax.rem(y + d, ny)}).start()
+
+    def weights_over_z():
+        wait_bytes(wy.at[pl.ds(0, ny - 1)], st_recv.at[4])
+        here = wy[0]
+        for d in range(1, ny):
+            here += wy[d]
+        wz[z] = here
+        for d in range(1, nz):
+            remote(wz.at[z], wz.at[z], st_send.at[5], st_recv.at[5], {Z: to_z(d)}).start()
+
     started = set()
-    for what, *of in plan(half, groups, LAG, BATCHES):
+    for what, *of in plan(half, groups, LAG, SENDS, BATCHES):
         if what == "first":
             for way in range(2):
                 ring_copy(way, of[0], 0).start()
         elif what == "acts":
-            for h in range(1, half):
-                send_acts(to_z(h), h - 1, 0, a2a_send.at[0], a2a_recv.at[h - 1])
-                send_acts(to_z(nz - h), h - 1, 1, a2a_send.at[0], a2a_recv.at[h - 1])
-            send_acts(to_z(half), far, 1, a2a_send.at[1], a2a_recv.at[far])
+            for i in of[0]:
+                if i == far:
+                    send_acts(to_z(half), far, 1, a2a_send.at[1], a2a_recv.at[far])
+                else:
+                    send_acts(to_z(i + 1), i, 0, a2a_send.at[0], a2a_recv.at[i])
+                    send_acts(to_z(nz - 1 - i), i, 1, a2a_send.at[0], a2a_recv.at[i])
+        elif what == "weights":
+            weights_over_y()
         elif what == "hop":
             g, h = of
+            if h == half - 1 and g == 0:
+                weights_over_z()
             for way in range(2):
                 if h <= last_hop(way, g):
                     wait_bytes(G.at[g, 0, 0], ring_recv.at[way, g, h - 1])
@@ -183,74 +210,83 @@
                 started.add(g)
         elif what == "scatter":
             g = of[0]
-            for d in range(1, ny):
+            for d in ys:
                 there = lax.rem(y + d, ny)
                 remote(part.at[g, there], R.at[g, d - 1], y_send.at[0], y_recv.at[g], {Y: there}).start()
 
     row_sq = jnp.zeros((1, LANE), jnp.float32)
     for g in range(groups):
+        if g == groups - 1:
+            wait_bytes(A.at[pl.ds(0, half - 1), :, pl.ds(0, share), :], a2a_send.at[0])
+            wait_bytes(A.at[0, 0, pl.ds(0, share), :], a2a_send.at[1])
+            wait_bytes(A.at[pl.ds(0, half - 1), :, pl.ds(0, share * (nx - 1)), :], x_send.at[0])
+            wait_bytes(A.at[0, 0, pl.ds(0, share * (nx - 1)), :], x_send.at[1])
+            wait_bytes(A.at[pl.ds(0, half - 1), :, pl.ds(0, core_rows), :], d_send.at[0])
+            wait_bytes(A.at[0, 0, pl.ds(0, core_rows), :], d_send.at[1])
+            for way in range(2):
+                wait_bytes(G.at[0], ring_send.at[way, 0])
+                wait_bytes(G.at[0, pl.ds(0, half - 1)], ring_send.at[way, 1])
+            wait_bytes(wy.at[pl.ds(0, ny - 1)], st_send.at[4])
+            wait_bytes(wz.at[pl.ds(0, nz - 1)], st_send.at[5])
+            wait_bytes(wz.at[pl.ds(0, nz - 1)], st_recv.at[5])
         wait_bytes(R.at[0], y_recv.at[g])
         total = part[g, y]
         for d in range(ny - 1):
             total += R[g, d]
         row_sq += jnp.sum(total * total + floor_eps, axis=0, keepdims=True)
-        grad[:, g * LANE:(g + 1) * LANE] = total.T
+        if g < groups - 1:
+            grad[:, g * LANE:(g + 1) * LANE] = total.T
 
     st1[xc] = jnp.broadcast_to(row_sq, (8, LANE))
-    for k in range(1, nx * nc):
+    for k in peers:
         remote(st1.at[xc], st1.at[xc], st_send.at[0], st_recv.at[0], col_peer(k)).start()
+    grad[:, (groups - 1) * LANE:] = total.T
     for g in range(groups):
         grads = grad[:, g * LANE:(g + 1) * LANE]
         st2[y, g:g + 1, :] = jnp.sum(grads * grads + floor_eps, axis=0, keepdims=True)
-    wait_bytes(A.at[pl.ds(0, half - 1), :, pl.ds(0, share), :], a2a_send.at[0])
-    wait_bytes(A.at[0, 0, pl.ds(0, share), :], a2a_send.at[1])
-    wait_bytes(A.at[pl.ds(0, half - 1), :, pl.ds(0, share * (nx - 1)), :], x_send.at[0])
-    wait_bytes(A.at[0, 0, pl.ds(0, share * (nx - 1)), :], x_send.at[1])
-    wait_bytes(A.at[pl.ds(0, half - 1), :, pl.ds(0, core_rows), :], d_send.at[0])
-    wait_bytes(A.at[0, 0, pl.ds(0, core_rows), :], d_send.at[1])
-    for way in range(2):
-        wait_bytes(G.at[0], ring_send.at[way, 0])
-        wait_bytes(G.at[0, pl.ds(0, half - 1)], ring_send.at[way, 1])
+    weight_total = wz[0]
+    for d in range(1, nz):
+        weight_total += wz[d]
+    st4[xc, 4:8, :] = jnp.broadcast_to(weight_total, (4, LANE))
     wait_bytes(part.at[:, pl.ds(0, ny - 1)], y_send.at[0])
+    wait_bytes(st1.at[pl.ds(0, nx * nc - 1)], st_send.at[0])
 
     wait_bytes(st1.at[pl.ds(0, nx * nc - 1)], st_recv.at[0])
     row_total = st1[0, 0:1, :]
     for k in range(1, nx * nc):
         row_total += st1[k, 0:1, :]
     row_moment = decay_rate * rs_v[...] + (1.0 - decay_rate) * (row_total / cols_all)
-    row_out[...] = row_moment
-    rows_down = jnp.broadcast_to(row_moment, (LANE, LANE)).T
-    inverse = 1.0 / rows_down
+    inverse = jnp.broadcast_to(1.0 / row_moment, (LANE, LANE)).T
     for g in range(groups):
         grads = grad[:, g * LANE:(g + 1) * LANE]
         st2[y, 4 + g:5 + g, :] = jnp.sum(grads * grads * inverse, axis=0, keepdims=True)
 
-    for d in range(1, ny):
+    for d in ys:
         remote(st2.at[y], st2.at[y], st_send.at[1], st_recv.at[1], {Y: lax.rem(y + d, ny)}).start()
-    wait_bytes(st1.at[pl.ds(0, nx * nc - 1)], st_send.at[0])
+    row_out[...] = row_moment
+    rows_down = jnp.broadcast_to(row_moment, (LANE, LANE)).T
+    wait_bytes(st2.at[pl.ds(0, ny - 1)], st_send.at[1])
     wait_bytes(st2.at[pl.ds(0, ny - 1)], st_recv.at[1])
     over_y = st2[0]
     for d in range(1, ny):
         over_y += st2[d]
     st3[z] = over_y
-    for d in sorted(range(1, nz), key=lambda d: -min(d, nz - d)):
+    for d in zs:
         remote(st3.at[z], st3.at[z], st_send.at[2], st_recv.at[2], {Z: to_z(d)}).start()
-    wait_bytes(st2.at[pl.ds(0, ny - 1)], st_send.at[1])
+    wait_bytes(st3.at[pl.ds(0, nz - 1)], st_send.at[2])
     wait_bytes(st3.at[pl.ds(0, nz - 1)], st_recv.at[2])
     over_z = st3[0]
     for d in range(1, nz):
         over_z += st3[d]
     col_moment = decay_rate * cs_v[...] + (1.0 - decay_rate) * (over_z[0:groups] / width)
     st4[xc, 0:4, :] = over_z[4:4 + groups] / col_moment
-    st4[xc, 4:8, :] = over_z[8:12]
-
-    for k in range(1, nx * nc):
+
+    for k in peers:
         remote(st4.at[xc], st4.at[xc], st_send.at[3], st_recv.at[3], col_peer(k)).start()
     col_out[...] = col_moment
     for g in range(groups):
         lanes = slice(g * LANE, (g + 1) * LANE)
         unclipped_out[:, lanes] = grad[:, lanes] * lax.rsqrt(rows_down * col_moment[g:g + 1, :])
-    wait_bytes(st3.at[pl.ds(0, nz - 1)], st_send.at[2])
     wait_bytes(st4.at[pl.ds(0, nx * nc - 1)], st_recv.at[3])
     over_x = st4[0]
     for k in range(1, nx * nc):
@@ -260,6 +296,16 @@
     clip_out[...] = jnp.broadcast_to(jnp.maximum(1.0, jnp.sqrt(update_total / count_all)), clip_out.shape)
     step_out[...] = jnp.broadcast_to(relative_rate * jnp.sqrt(weight_total / count_all + 1e-06), step_out.shape)
     wait_bytes(st4.at[pl.ds(0, nx * nc - 1)], st_send.at[3])
+
+
+def finish(unclipped, weight, row_moment, col_moment, clip_factor, step_size, new_weight, update, row_out, col_out):
+    row_out[...] = row_moment[...]
+    col_out[...] = col_moment[...]
+    for g in range(col_moment.shape[0]):
+        lanes = slice(g * LANE, (g + 1) * LANE)
+        clipped = unclipped[:, lanes] / clip_factor[g:g + 1, :]
+        update[:, lanes] = clipped
+        new_weight[:, lanes] = weight[:, lanes] - step_size[g:g + 1, :] * clipped
 
 
 def per_device(acts, out_grads, weight, row_state, col_state):
@@ -293,9 +339,11 @@
             pltpu.VMEM((1, LANE), f32),
             pltpu.VMEM((groups, LANE), f32),
             pltpu.VMEM((nx * nc, 8, LANE), f32),
-            pltpu.VMEM((ny, 16, LANE), f32),
-            pltpu.VMEM((nz, 16, LANE), f32),
+            pltpu.VMEM((ny, 8, LANE), f32),
+            pltpu.VMEM((nz, 8, LANE), f32),
             pltpu.VMEM((nx * nc, 8, LANE), f32),
+            pltpu.VMEM((ny, 1, LANE), f32),
+            pltpu.VMEM((nz, 1, LANE), f32),
             pltpu.SemaphoreType.DMA((groups + 4,)),
             pltpu.SemaphoreType.DMA((2,)),
             pltpu.SemaphoreType.DMA((half,)),
@@ -307,15 +355,24 @@
             pltpu.SemaphoreType.DMA((2, groups, half)),
             pltpu.SemaphoreType.DMA((1,)),
             pltpu.SemaphoreType.DMA((groups,)),
-            pltpu.SemaphoreType.DMA((4,)),
-            pltpu.SemaphoreType.DMA((4,)),
+            pltpu.SemaphoreType.DMA((6,)),
+            pltpu.SemaphoreType.DMA((6,)),
         ],
         compiler_params=pltpu.CompilerParams(
             collective_id=0, has_side_effects=True, vmem_limit_bytes=60 * 1024 * 1024
         ),
     )(acts, out_grads, weight, row_state.reshape(1, LANE), col_state.reshape(groups, LANE))
-    update = unclipped / clip_factor.reshape(1, -1)
-    new_weight = weight - step_size.reshape(1, -1) * update
+    new_weight, update, row_moment, col_moment = pl.pallas_call(
+        finish,
+        out_shape=(
+            jax.ShapeDtypeStruct((LANE, cols), f32),
+            jax.ShapeDtypeStruct((LANE, cols), f32),
+            jax.ShapeDtypeStruct((1, LANE), f32),
+            jax.ShapeDtypeStruct((groups, LANE), f32),
+        ),
+        in_specs=[vmem] * 6,
+        out_specs=[vmem] * 4,
+    )(unclipped, weight, row_moment, col_moment, clip_factor, step_size)
     return (new_weight, update, row_moment.reshape(-1), col_moment.reshape(-1))
 
 

time: 94.4 us -> 88.7 us (0.940)
  local copies, waits for them, and re-layouts: 2.38 us -> 0 us
  other arithmetic: 1.82 us -> 0 us
  Pallas kernels: 89.4 us -> 87.9 us
    pallas_call x1, Pallas kernels: 89.4 us -> 86 us  [per_device(): pl.pallas_call(functools.partial(kernel, (nz, ny, nx, nc, tok, cols, widt...]
    unnamed x4 -> x0, local copies, waits for them, and re-layouts: 2.38 us -> none
    pallas_call x0 -> x1, Pallas kernels: none -> 1.88 us  [per_device(): pl.pallas_call(finish, out_shape=(jax.ShapeDtypeStruct((LANE, cols), f32)...]
    sub x1 -> x0, other arithmetic: 1.82 us -> none  [per_device(): new_weight = weight - step_size.reshape(1, -1) * update]
where the time goes in v4:
time: 88.7 us; the launch traced here: 88.5 us
  Pallas kernels  87.9 us (99%)
    pallas_call x1, Pallas kernels, per_device(): pl.pallas_call(functools.partial(kernel, (nz, ny, nx, nc, tok, cols, widt...  86 us
    pallas_call x1, Pallas kernels, per_device(): pl.pallas_call(finish, out_shape=(jax.ShapeDtypeStruct((LANE, cols), f32)...  1.88 us

profile of v4, /device:TPU:1, one launch (start us, length us, event | category | flops | bytes accessed | tf_op | source)
XLA Modules:
  0.0 88.5 jit_solution(9144700500115645782)
XLA Ops:
  0.6 86.0 %shard_map.84 = (f32[128,512]{1,0:T(8,128)}, f32[1,128]{1,0:T(1,128)}, f32[4,128]{1,0:T(4,128)}, f32[4,128]{1,0:T(4,128)}, f32[4,128]{1,0:T(4,128)}) custom-call(bf16[128,8192]{1,0:T(8,128)(2,1)} %acts.1, bf16[128,512]{1,0:T(8,128)(2,1)} %og.1, f32[128,512]{1,0:T(8,128)} %weight.3, f32[1,128]{1,0:T(1,128)} %bitcast.5, f32[4,128]{1,0:T(4,128)} %bitcast.4), custom_call_target="tpu_custom_call" | custom-call | tf_op jit(solution)/shard_map/pallas_call | solution.py:321
  86.7 1.9 %shard_map.85 = (f32[128,512]{1,0:T(8,128)}, f32[128,512]{1,0:T(8,128)}, f32[1,128]{1,0:T(1,128)}, f32[4,128]{1,0:T(4,128)}) custom-call(f32[128,512]{1,0:T(8,128)} %get-tuple-element.13.unclipped, f32[128,512]{1,0:T(8,128)} %weight.3, f32[1,128]{1,0:T(1,128)} %get-tuple-element.14.row_moment, f32[4,128]{1,0:T(4,128)} %get-tuple-element.15.col_moment, ...), custom_call_target="tpu_custom_call" | custom-call | tf_op jit(solution)/shard_map/pallas_call | solution.py:365

commit v5 on v4

--- a/solution.py
+++ b/solution.py
@@ -12,9 +12,9 @@
 ROW = (Z, Y)
 COL = (X, C)
 LANE = 128
-LAG = (0, 0, 1, 1)
-SENDS = (([7], 0), ([6, 5], 0), ([4, 3], 1), ([2, 1, 0], 2))
-BATCHES = (([7], 2), ([5, 6], 2), ([3, 4], 3), ([0, 1, 2], 4))
+LAG = (0, 0, 1, 2)
+SENDS = (([7], 0), ([6], 1), ([5], 1), ([4], 2), ([3], 2), ([2], 2), ([1], 3), ([0], 3))
+BATCHES = (([7], 2), ([5, 6], 3), ([2, 3, 4], 4), ([0, 1], 5))
 
 decay_rate = 0.85
 floor_eps = 1e-30
@@ -28,6 +28,15 @@
     steps += [("first", g) for g in range(groups) if lag[g] == 1]
     ready, done = [], {g: [] for g in range(groups)}
     arrived = {g: [] for g in range(groups)}
+
+    def multiply(g):
+        todo = [i for i in arrived[g] if i in ready and i not in done[g]]
+        done[g] += todo
+        if todo:
+            steps.append(("dot", g, todo))
+        if len(done[g]) == half:
+            steps.append(("scatter", g))
+
     for r in range(1, half + max(lag) + 1):
         for g in range(groups):
             if lag[g] == r and r > 1:
@@ -36,6 +45,8 @@
             if 1 <= h <= half:
                 steps.append(("hop", g, h))
                 arrived[g].append(h - 1)
+                if h == half and len(ready) == half:
+                    multiply(g)
         steps += [("acts", pairs) for pairs, at in sends if at == r]
         for stage in (1, 2, 3):
             for pairs, at in batches:
@@ -44,13 +55,9 @@
                     if stage == 3:
                         ready += pairs
         for g in range(groups):
-            todo = [i for i in arrived[g] if i in ready and i not in done[g]]
-            done[g] += todo
-            if todo:
-                steps.append(("dot", g, todo))
-            if r - lag[g] == half:
-                assert len(done[g]) == half
-                steps.append(("scatter", g))
+            if len(done[g]) < half:
+                multiply(g)
+    assert all(len(done[g]) == half for g in range(groups))
     return steps
 
 
@@ -188,8 +195,6 @@
             weights_over_y()
         elif what == "hop":
             g, h = of
-            if h == half - 1 and g == 0:
-                weights_over_z()
             for way in range(2):
                 if h <= last_hop(way, g):
                     wait_bytes(G.at[g, 0, 0], ring_recv.at[way, g, h - 1])
@@ -214,6 +219,8 @@
                 there = lax.rem(y + d, ny)
                 remote(part.at[g, there], R.at[g, d - 1], y_send.at[0], y_recv.at[g], {Y: there}).start()
 
+    weights_over_z()
+
     row_sq = jnp.zeros((1, LANE), jnp.float32)
     for g in range(groups):
         if g == groups - 1:
@@ -227,8 +234,6 @@
                 wait_bytes(G.at[0], ring_send.at[way, 0])
                 wait_bytes(G.at[0, pl.ds(0, half - 1)], ring_send.at[way, 1])
             wait_bytes(wy.at[pl.ds(0, ny - 1)], st_send.at[4])
-            wait_bytes(wz.at[pl.ds(0, nz - 1)], st_send.at[5])
-            wait_bytes(wz.at[pl.ds(0, nz - 1)], st_recv.at[5])
         wait_bytes(R.at[0], y_recv.at[g])
         total = part[g, y]
         for d in range(ny - 1):
@@ -244,10 +249,6 @@
     for g in range(groups):
         grads = grad[:, g * LANE:(g + 1) * LANE]
         st2[y, g:g + 1, :] = jnp.sum(grads * grads + floor_eps, axis=0, keepdims=True)
-    weight_total = wz[0]
-    for d in range(1, nz):
-        weight_total += wz[d]
-    st4[xc, 4:8, :] = jnp.broadcast_to(weight_total, (4, LANE))
     wait_bytes(part.at[:, pl.ds(0, ny - 1)], y_send.at[0])
     wait_bytes(st1.at[pl.ds(0, nx * nc - 1)], st_send.at[0])
 
@@ -273,6 +274,12 @@
     st3[z] = over_y
     for d in zs:
         remote(st3.at[z], st3.at[z], st_send.at[2], st_recv.at[2], {Z: to_z(d)}).start()
+    wait_bytes(wz.at[pl.ds(0, nz - 1)], st_send.at[5])
+    wait_bytes(wz.at[pl.ds(0, nz - 1)], st_recv.at[5])
+    weight_total = wz[0]
+    for d in range(1, nz):
+        weight_total += wz[d]
+    st4[xc, 4:8, :] = jnp.broadcast_to(weight_total, (4, LANE))
     wait_bytes(st3.at[pl.ds(0, nz - 1)], st_send.at[2])
     wait_bytes(st3.at[pl.ds(0, nz - 1)], st_recv.at[2])
     over_z = st3[0]
@@ -286,7 +293,9 @@
     col_out[...] = col_moment
     for g in range(groups):
         lanes = slice(g * LANE, (g + 1) * LANE)
-        unclipped_out[:, lanes] = grad[:, lanes] * lax.rsqrt(rows_down * col_moment[g:g + 1, :])
+        grad[:, lanes] = grad[:, lanes] * lax.rsqrt(rows_down * col_moment[g:g + 1, :])
+    leaving = pltpu.make_async_copy(grad, unclipped_out, local_sem.at[0])
+    leaving.start()
     wait_bytes(st4.at[pl.ds(0, nx * nc - 1)], st_recv.at[3])
     over_x = st4[0]
     for k in range(1, nx * nc):
@@ -296,6 +305,7 @@
     clip_out[...] = jnp.broadcast_to(jnp.maximum(1.0, jnp.sqrt(update_total / count_all)), clip_out.shape)
     step_out[...] = jnp.broadcast_to(relative_rate * jnp.sqrt(weight_total / count_all + 1e-06), step_out.shape)
     wait_bytes(st4.at[pl.ds(0, nx * nc - 1)], st_send.at[3])
+    leaving.wait()
 
 
 def finish(unclipped, weight, row_moment, col_moment, clip_factor, step_size, new_weight, update, row_out, col_out):
@@ -328,7 +338,7 @@
             jax.ShapeDtypeStruct((groups, LANE), f32),
         ),
         in_specs=[anywhere] * 5,
-        out_specs=[vmem] * 5,
+        out_specs=[anywhere] + [vmem] * 4,
         scratch_shapes=[
             pltpu.VMEM((half, 2, tok, rows_z), jnp.bfloat16),
             pltpu.VMEM((groups, half, 2, tok, LANE), jnp.bfloat16),

time: 88.7 us -> 86.6 us (0.976)
  Pallas kernels: 87.9 us -> 85.8 us
    pallas_call x1, Pallas kernels: 86 us -> 83.9 us  [per_device(): pl.pallas_call(functools.partial(kernel, (nz, ny, nx, nc, tok, cols, widt...]
where the time goes in v5:
time: 86.6 us; the launch traced here: 86.4 us
  Pallas kernels  85.8 us (99%)
    pallas_call x1, Pallas kernels, per_device(): pl.pallas_call(functools.partial(kernel, (nz, ny, nx, nc, tok, cols, widt...  83.9 us
    pallas_call x1, Pallas kernels, per_device(): pl.pallas_call(finish, out_shape=(jax.ShapeDtypeStruct((LANE, cols), f32)...  1.88 us

profile of v5, /device:TPU:1, one launch (start us, length us, event | category | flops | bytes accessed | tf_op | source)
XLA Modules:
  0.0 86.4 jit_solution(15844684738496611931)
XLA Ops:
  0.6 83.9 %shard_map.84 = (f32[128,512]{1,0:T(8,128)}, f32[1,128]{1,0:T(1,128)}, f32[4,128]{1,0:T(4,128)}, f32[4,128]{1,0:T(4,128)}, f32[4,128]{1,0:T(4,128)}) custom-call(bf16[128,8192]{1,0:T(8,128)(2,1)} %acts.1, bf16[128,512]{1,0:T(8,128)(2,1)} %og.1, f32[128,512]{1,0:T(8,128)} %weight.3, f32[1,128]{1,0:T(1,128)} %bitcast.5, f32[4,128]{1,0:T(4,128)} %bitcast.4), custom_call_target="tpu_custom_call" | custom-call | tf_op jit(solution)/shard_map/pallas_call | solution.py:331
  84.5 1.9 %shard_map.85 = (f32[128,512]{1,0:T(8,128)}, f32[128,512]{1,0:T(8,128)}, f32[1,128]{1,0:T(1,128)}, f32[4,128]{1,0:T(4,128)}) custom-call(f32[128,512]{1,0:T(8,128)} %get-tuple-element.13.unclipped, f32[128,512]{1,0:T(8,128)} %weight.3, f32[1,128]{1,0:T(1,128)} %get-tuple-element.14.row_moment, f32[4,128]{1,0:T(4,128)} %get-tuple-element.15.col_moment, ...), custom_call_target="tpu_custom_call" | custom-call | tf_op jit(solution)/shard_map/pallas_call | solution.py:375

commit v6 on v5

--- a/solution.py
+++ b/solution.py
@@ -219,8 +219,6 @@
                 there = lax.rem(y + d, ny)
                 remote(part.at[g, there], R.at[g, d - 1], y_send.at[0], y_recv.at[g], {Y: there}).start()
 
-    weights_over_z()
-
     row_sq = jnp.zeros((1, LANE), jnp.float32)
     for g in range(groups):
         if g == groups - 1:
@@ -233,7 +231,6 @@
             for way in range(2):
                 wait_bytes(G.at[0], ring_send.at[way, 0])
                 wait_bytes(G.at[0, pl.ds(0, half - 1)], ring_send.at[way, 1])
-            wait_bytes(wy.at[pl.ds(0, ny - 1)], st_send.at[4])
         wait_bytes(R.at[0], y_recv.at[g])
         total = part[g, y]
         for d in range(ny - 1):
@@ -242,20 +239,22 @@
         if g < groups - 1:
             grad[:, g * LANE:(g + 1) * LANE] = total.T
 
-    st1[xc] = jnp.broadcast_to(row_sq, (8, LANE))
+    st1[xc] = row_sq
     for k in peers:
         remote(st1.at[xc], st1.at[xc], st_send.at[0], st_recv.at[0], col_peer(k)).start()
     grad[:, (groups - 1) * LANE:] = total.T
     for g in range(groups):
         grads = grad[:, g * LANE:(g + 1) * LANE]
         st2[y, g:g + 1, :] = jnp.sum(grads * grads + floor_eps, axis=0, keepdims=True)
+    weights_over_z()
+    wait_bytes(wy.at[pl.ds(0, ny - 1)], st_send.at[4])
     wait_bytes(part.at[:, pl.ds(0, ny - 1)], y_send.at[0])
     wait_bytes(st1.at[pl.ds(0, nx * nc - 1)], st_send.at[0])
 
     wait_bytes(st1.at[pl.ds(0, nx * nc - 1)], st_recv.at[0])
-    row_total = st1[0, 0:1, :]
+    row_total = st1[0]
     for k in range(1, nx * nc):
-        row_total += st1[k, 0:1, :]
+        row_total += st1[k]
     row_moment = decay_rate * rs_v[...] + (1.0 - decay_rate) * (row_total / cols_all)
     inverse = jnp.broadcast_to(1.0 / row_moment, (LANE, LANE)).T
     for g in range(groups):
@@ -348,7 +347,7 @@
             pltpu.VMEM((LANE, cols), f32),
             pltpu.VMEM((1, LANE), f32),
             pltpu.VMEM((groups, LANE), f32),
-            pltpu.VMEM((nx * nc, 8, LANE), f32),
+            pltpu.VMEM((nx * nc, 1, LANE), f32),
             pltpu.VMEM((ny, 8, LANE), f32),
             pltpu.VMEM((nz, 8, LANE), f32),
             pltpu.VMEM((nx * nc, 8, LANE), f32),

time: 86.6 us -> 86.5 us (level)
  no operation moved by 1% of the time
where the time goes in v6:
time: 86.5 us; the launch traced here: 86.3 us
  Pallas kernels  85.7 us (99%)
    pallas_call x1, Pallas kernels, per_device(): pl.pallas_call(functools.partial(kernel, (nz, ny, nx, nc, tok, cols, widt...  83.8 us
    pallas_call x1, Pallas kernels, per_device(): pl.pallas_call(finish, out_shape=(jax.ShapeDtypeStruct((LANE, cols), f32)...  1.88 us

profile of v6, /device:TPU:1, one launch (start us, length us, event | category | flops | bytes accessed | tf_op | source)
XLA Modules:
  0.0 86.3 jit_solution(6678303368904756491)
XLA Ops:
  0.6 83.8 %shard_map.84 = (f32[128,512]{1,0:T(8,128)}, f32[1,128]{1,0:T(1,128)}, f32[4,128]{1,0:T(4,128)}, f32[4,128]{1,0:T(4,128)}, f32[4,128]{1,0:T(4,128)}) custom-call(bf16[128,8192]{1,0:T(8,128)(2,1)} %acts.1, bf16[128,512]{1,0:T(8,128)(2,1)} %og.1, f32[128,512]{1,0:T(8,128)} %weight.3, f32[1,128]{1,0:T(1,128)} %bitcast.5, f32[4,128]{1,0:T(4,128)} %bitcast.4), custom_call_target="tpu_custom_call" | custom-call | tf_op jit(solution)/shard_map/pallas_call | solution.py:330
  84.5 1.9 %shard_map.85 = (f32[128,512]{1,0:T(8,128)}, f32[128,512]{1,0:T(8,128)}, f32[1,128]{1,0:T(1,128)}, f32[4,128]{1,0:T(4,128)}) custom-call(f32[128,512]{1,0:T(8,128)} %get-tuple-element.13.unclipped, f32[128,512]{1,0:T(8,128)} %weight.3, f32[1,128]{1,0:T(1,128)} %get-tuple-element.14.row_moment, f32[4,128]{1,0:T(4,128)} %get-tuple-element.15.col_moment, ...), custom_call_target="tpu_custom_call" | custom-call | tf_op jit(solution)/shard_map/pallas_call | solution.py:374
